TPU v7x, 512 devices: a whole 4x8x8 slice. The times are simulated.
512 devices in a mesh: section: 8 (over z_hi, core), expert: 64 (over z_lo, x, y).
Axes of the slice: x: 4, y: 8, z: 8 (z_hi: 4, z_lo: 2; z = z_hi * 2 + z_lo), core: 2. Of those that a mesh axis runs over, the one named last changes fastest.
Arguments:
- tokens_forward: bfloat16 [8, 2560, 2048], P('section', 'expert'), may hold values from -6 to 6
- tokens_reverse: bfloat16 [8, 2560, 2048], P('section', 'expert'), may hold values from -6 to 6
- routes_forward: int32 [8, 2560, 8], P('section', 'expert'), may hold values from 0 to 63, all different within a row; in each aligned block of 40 rows (0 to 39, 40 to 79, ..., all dimensions but the last counted through in order) at most 7 rows name the same one
- routes_reverse: int32 [8, 2560, 8], P('section', 'expert'), may hold values from 0 to 63, all different within a row; in each aligned block of 40 rows (0 to 39, 40 to 79, ..., all dimensions but the last counted through in order) at most 7 rows name the same one
- hidden_forward: bfloat16 [8, 64, 448, 768], P('section', 'expert'), may hold values from -6 to 6
- hidden_reverse: bfloat16 [8, 64, 448, 768], P('section', 'expert'), may hold values from -6 to 6
- router_weight: bfloat16 [8, 2048, 64], P('section'), may hold values from -0.125 to 0.125
- down_weight: bfloat16 [8, 64, 768, 2048], P('section', 'expert'), may hold values from -0.21875 to 0.21875
Outputs:
- arrived_forward: bfloat16 [8, 2560, 2048], P('section', 'expert')
- arrived_reverse: bfloat16 [8, 2560, 2048], P('section', 'expert')
Inputs may be any that keep to these rules, and one draw needn't show every extreme that they name: `routes_forward`: the 8 experts of a token differ. The 40 tokens of one device (aligned blocks of rows at one section) name no expert more than 7 times in all, and in some device's tokens an expert is named exactly 7 times. `routes_reverse`: as for routes_forward.
All inputs are finite; a program needn't handle non-finite values.
Results may differ from a plain program's by a relative error of at most 0.0029.
Values may be sent and summed in bfloat16 or wider, within the bound.
No kernel may reach another device: no remote copies, remote signals or barrier semaphores. Data moves between devices by JAX's collectives and lax.ppermute only.
A program may use at most 64 MiB of HBM per device.

v0:
```python
import jax
import jax.numpy as jnp
from jax import lax
from jax.sharding import PartitionSpec as P


def passed_along(block, axis, distance):
    devices = range(lax.axis_size(axis))
    route = [((i - distance) % len(devices), i) for i in devices]
    return lax.ppermute(block, axis, route)


def route_slots(tokens, routes, router, capacity):
    experts = router.shape[1]
    logits = jnp.dot(tokens, router, preferred_element_type=jnp.float32)
    expert_ids = jnp.arange(experts, dtype=jnp.int32)
    chosen = jnp.sum(
        jnp.where(routes[:, :, None] == expert_ids[None, None, :], logits[:, None, :], 0.0), axis=2
    )
    raised = jnp.exp(chosen)
    gate_share = raised / jnp.sum(raised, axis=1, keepdims=True)
    flat_ids = routes.reshape(-1)
    one_hot = (flat_ids[:, None] == expert_ids[None, :]).astype(jnp.int32)
    slot_rank = jnp.sum((jnp.cumsum(one_hot, axis=0) - one_hot) * one_hot, axis=1)
    return (gate_share, flat_ids * capacity + slot_rank)


def expert_rows(hidden, down_w, experts, capacity):
    expert_out = jnp.dot(hidden, down_w, preferred_element_type=jnp.float32)
    return expert_out.astype(jnp.bfloat16).reshape(experts, capacity, down_w.shape[1])


def send_back(rows):
    return lax.all_to_all(rows, "expert", split_axis=0, concat_axis=0, tiled=True)


def collect_rows(returned, gate_share, slot_index):
    flattened = returned.reshape(-1, returned.shape[2])
    picked = flattened[slot_index].reshape(
        gate_share.shape[0], gate_share.shape[1], returned.shape[2]
    )
    return jnp.sum(gate_share[:, :, None] * picked.astype(jnp.float32), axis=1)


def shards(
    tokens_forward,
    tokens_reverse,
    routes_forward,
    routes_reverse,
    hidden_forward,
    hidden_reverse,
    router_weight,
    down_weight,
):
    down_w = down_weight[0, 0]
    router = router_weight[0]
    experts = router.shape[1]
    capacity = hidden_forward.shape[2] // experts
    rising = tokens_forward[0]
    falling = tokens_reverse[0]
    rising_gate, rising_slots = route_slots(rising, routes_forward[0], router, capacity)
    falling_gate, falling_slots = route_slots(falling, routes_reverse[0], router, capacity)
    rising_rows = expert_rows(hidden_forward[0, 0], down_w, experts, capacity)
    rising_back = send_back(rising_rows)
    falling_rows = expert_rows(hidden_reverse[0, 0], down_w, experts, capacity)
    falling_back = send_back(falling_rows)
    rising_sum = collect_rows(rising_back, rising_gate, rising_slots)
    falling_sum = collect_rows(falling_back, falling_gate, falling_slots)
    rising_layer = (rising.astype(jnp.float32) + rising_sum).astype(jnp.bfloat16)
    falling_layer = (falling.astype(jnp.float32) + falling_sum).astype(jnp.bfloat16)
    rising_next = passed_along(rising_layer, "section", 1)
    falling_next = passed_along(falling_layer, "section", -1)
    return (rising_next[None], falling_next[None])


def solution(mesh):
    in_specs = (
        P("section", "expert", None),
        P("section", "expert", None),
        P("section", "expert", None),
        P("section", "expert", None),
        P("section", "expert", None, None),
        P("section", "expert", None, None),
        P("section", None, None),
        P("section", "expert", None, None),
    )
    out_specs = (P("section", "expert", None), P("section", "expert", None))
    return jax.shard_map(shards, mesh=mesh, in_specs=in_specs, out_specs=out_specs, check_vma=False)
```

profile of v0, /device:TPU:1, one launch (start us, length us, event | category | flops | bytes accessed | tf_op | source)
XLA Modules:
  0.0 158.2 jit_solution(7889271714473207287)
XLA Ops:
  0.6 1.9 %copy-done = bf16[1,1,768,2048]{3,2,1,0:T(8,128)(2,1)S(1)} copy-done((bf16[1,1,768,2048]{3,2,1,0:T(8,128)(2,1)S(1)}, bf16[1,1,768,2048]{3,2,1,0:T(8,128)(2,1)}, u32[]{:S(2)}) %copy-start) | copy-done | bytes 3145752
  2.5 3.9 %fusion.4 = bf16[448,2048]{1,0:T(8,128)(2,1)} fusion(bf16[1,1,768,2048]{3,2,1,0:T(8,128)(2,1)S(1)} %copy-done, bf16[1,1,448,768]{3,2,1,0:T(8,128)(2,1)} %param.12), kind=kOutput, calls=%fused_computation.6 | convolution fusion | flops 1410203648 | bytes 5668864 | tf_op jit(solution)/shard_map/dot_general | solution.py:29
  6.5 3.7 %reshape.144 = bf16[64,7,2048]{2,1,0:T(8,128)(2,1)} reshape(bf16[448,2048]{1,0:T(8,128)(2,1)} %fusion.4) | data formatting | bytes 3670016 | tf_op jit(solution)/shard_map/reshape | solution.py:30
  10.1 13.3 %all-to-all-start = ((bf16[64,7,2048]{2,1,0:T(8,128)(2,1)}), bf16[64,7,2048]{2,1,0:T(8,128)(2,1)}, u32[]{:S(2)}, u32[]{:S(2)}) async-start(bf16[64,7,2048]{2,1,0:T(8,128)(2,1)} %reshape.144), calls=%async_computation | async-start | bytes 4194304 | tf_op jit(solution)/shard_map/all_to_all | solution.py:34
  23.5 0.1 copy.24
  23.6 0.1 copy.23
  23.6 0.7 mul.50
  24.3 0.1 eq.78
  24.5 0.9 reduce-window.14
  25.4 0.2 slice_reduce_fusion.1
  25.6 0.6 reduce-window.15
  26.2 0.1 copy.22
  26.3 3.9 %fusion.7 = bf16[448,2048]{1,0:T(8,128)(2,1)} fusion(bf16[1,1,768,2048]{3,2,1,0:T(8,128)(2,1)S(1)} %copy-done, bf16[1,1,448,768]{3,2,1,0:T(8,128)(2,1)} %param.13), kind=kOutput, calls=%fused_computation.7 | convolution fusion | flops 1410203648 | bytes 5668864 | tf_op jit(solution)/shard_map/dot_general | solution.py:29
  30.2 3.7 %reshape.148 = bf16[64,7,2048]{2,1,0:T(8,128)(2,1)} reshape(bf16[448,2048]{1,0:T(8,128)(2,1)} %fusion.7) | data formatting | bytes 3670016 | tf_op jit(solution)/shard_map/reshape | solution.py:30
  34.0 0.1 copy.28
  34.1 0.7 mul.55
  34.7 0.1 eq.89
  34.9 37.1 %all-to-all-done = bf16[64,7,2048]{2,1,0:T(8,128)(2,1)} async-done(((bf16[64,7,2048]{2,1,0:T(8,128)(2,1)}), bf16[64,7,2048]{2,1,0:T(8,128)(2,1)}, u32[]{:S(2)}, u32[]{:S(2)}) %all-to-all-start) | async-done | bytes 1835040 | tf_op jit(solution)/shard_map/all_to_all | solution.py:34
  71.9 8.2 %all-to-all-start.1 = ((bf16[64,7,2048]{2,1,0:T(8,128)(2,1)}), bf16[64,7,2048]{2,1,0:T(8,128)(2,1)}, u32[]{:S(2)}, u32[]{:S(2)}) async-start(bf16[64,7,2048]{2,1,0:T(8,128)(2,1)} %reshape.148), calls=%async_computation.1 | async-start | bytes 4194304 | tf_op jit(solution)/shard_map/all_to_all | solution.py:34
  80.1 0.6 copy_bitcast_fusion
  80.8 2.7 %reduce-window.16 = s32[64,3,128]{2,0,1:T(8,128)} reduce-window(s32[64,3,128]{2,0,1:T(8,128)} %copy_bitcast_fusion, s32[]{:T(128)} %constant.15.clone.1), window={size=1x1x128 pad=0_0x0_0x127_0}, to_apply=%region_8.9 | reduce-window | flops 3121152 | bytes 196612 | tf_op jit(solution)/shard_map/reduce-window.2
  83.5 1.1 slice_reduce_fusion
  84.6 0.6 reduce-window.19
  85.3 0.8 bitcast_bitcast_fusion.1
  86.1 0.7 fusion.24
  86.8 1.0 bitcast_bitcast_fusion
  87.8 0.7 fusion.21
  88.6 0.7 fusion.25
  89.3 1.1 fusion.16
  90.4 0.2 select_reduce_fusion.1
  90.6 0.1 exponential_reduce_fusion.1
  90.7 1.1 fusion.14
  91.8 0.2 select_reduce_fusion
  92.0 0.1 exponential_reduce_fusion
  92.1 0.1 exponential_divide_fusion.1
  92.2 0.1 exponential_divide_fusion
  92.3 3.8 %reshape.145 = bf16[448,2048]{1,0:T(8,128)(2,1)} reshape(bf16[64,7,2048]{2,1,0:T(8,128)(2,1)} %all-to-all-done) | data formatting | bytes 3670016 | tf_op jit(solution)/shard_map/reshape | solution.py:38
  96.1 6.7 %gather_fusion = bf16[320,2048]{1,0:T(8,128)(2,1)} fusion(bf16[448,2048]{1,0:T(8,128)(2,1)} %reshape.145, s32[1024]{0:T(1024)S(1)} %pad_clamp_fusion.1), kind=kCustom, calls=%fused_computation | custom fusion | bytes 2622720 | tf_op jit(solution)/shard_map/gather | solution.py:39
  102.8 2.6 %fusion.11 = f32[40,2048]{1,0:T(8,128)S(1)} fusion(bf16[320,2048]{1,0:T(8,128)(2,1)} %gather_fusion, f32[40,8]{1,0:T(8,128)S(1)} %exponential_divide_fusion.1), kind=kLoop, calls=%fused_computation.11 | loop fusion | flops 1884160 | bytes 1639680 | tf_op jit(solution)/shard_map/reduce_sum | solution.py:42
  105.5 7.7 %collective-permute-start = (bf16[40,2048]{1,0:T(8,128)(2,1)S(1)}, bf16[40,2048]{1,0:T(8,128)(2,1)}, u32[]{:S(2)}, u32[]{:S(2)}) collective-permute-start(bf16[40,2048]{1,0:T(8,128)(2,1)S(1)} %add_convert_fusion.1), channel_id=1, source_target_pairs={{448,0},{0,64},{64,128},{128,192},{192,256},{256,320},{320,384},{3... | collective-permute-start | bytes 491528 | tf_op jit(solution)/shard_map/ppermute | solution.py:10
  113.2 14.5 %all-to-all-done.1 = bf16[64,7,2048]{2,1,0:T(8,128)(2,1)} async-done(((bf16[64,7,2048]{2,1,0:T(8,128)(2,1)}), bf16[64,7,2048]{2,1,0:T(8,128)(2,1)}, u32[]{:S(2)}, u32[]{:S(2)}) %all-to-all-start.1) | async-done | bytes 1835040 | tf_op jit(solution)/shard_map/all_to_all | solution.py:34
  127.7 3.8 %reshape.149 = bf16[448,2048]{1,0:T(8,128)(2,1)} reshape(bf16[64,7,2048]{2,1,0:T(8,128)(2,1)} %all-to-all-done.1) | data formatting | bytes 3670016 | tf_op jit(solution)/shard_map/reshape | solution.py:38
  131.5 6.7 %gather_fusion.1 = bf16[320,2048]{1,0:T(8,128)(2,1)} fusion(bf16[448,2048]{1,0:T(8,128)(2,1)} %reshape.149, s32[1024]{0:T(1024)S(1)} %pad_clamp_fusion), kind=kCustom, calls=%fused_computation.1 | custom fusion | bytes 2622720 | tf_op jit(solution)/shard_map/gather | solution.py:39
  138.2 2.6 %fusion.10 = f32[40,2048]{1,0:T(8,128)S(1)} fusion(bf16[320,2048]{1,0:T(8,128)(2,1)} %gather_fusion.1, f32[40,8]{1,0:T(8,128)S(1)} %exponential_divide_fusion), kind=kLoop, calls=%fused_computation.9 | loop fusion | flops 1884160 | bytes 1639680 | tf_op jit(solution)/shard_map/reduce_sum | solution.py:42
  140.8 6.5 %collective-permute-start.1 = (bf16[40,2048]{1,0:T(8,128)(2,1)S(1)}, bf16[40,2048]{1,0:T(8,128)(2,1)S(1)}, u32[]{:S(2)}, u32[]{:S(2)}) collective-permute-start(bf16[40,2048]{1,0:T(8,128)(2,1)S(1)} %add_convert_fusion), channel_id=1, source_target_pairs={{64,0},{128,64},{192,128},{256,192},{320,256},{384,320},{448,384},... | collective-permute-start | bytes 491528 | tf_op jit(solution)/shard_map/ppermute | solution.py:10
  147.4 8.5 %collective-permute-done.1 = bf16[40,2048]{1,0:T(8,128)(2,1)S(1)} collective-permute-done((bf16[40,2048]{1,0:T(8,128)(2,1)S(1)}, bf16[40,2048]{1,0:T(8,128)(2,1)S(1)}, u32[]{:S(2)}, u32[]{:S(2)}) %collective-permute-start.1) | collective-permute-done | bytes 163872 | tf_op jit(solution)/shard_map/ppermute | solution.py:10
  155.9 1.6 %copy.42 = bf16[1,40,2048]{2,1,0:T(8,128)(2,1)} copy(bf16[1,40,2048]{2,1,0:T(8,128)(2,1)} %bitcast.7) | data formatting | bytes 327680
  157.5 0.7 copy.43
  (26 shorter events, 0.4 us)
Async XLA Ops:
  0.6 1.9 %copy-start = (bf16[1,1,768,2048]{3,2,1,0:T(8,128)(2,1)S(1)}, bf16[1,1,768,2048]{3,2,1,0:T(8,128)(2,1)}, u32[]{:S(2)}) copy-start(bf16[1,1,768,2048]{3,2,1,0:T(8,128)(2,1)} %param.15) | copy-start | bytes 9437188
  10.1 13.3 %copy-start.4 = (s32[1,40,8]{1,2,0:T(8,128)S(1)}, s32[1,40,8]{1,2,0:T(8,128)}, u32[]{:S(2)}) copy-start(s32[1,40,8]{1,2,0:T(8,128)} %param.10) | copy-start | bytes 3844
  10.1 61.8 %all-to-all-start = ((bf16[64,7,2048]{2,1,0:T(8,128)(2,1)}), bf16[64,7,2048]{2,1,0:T(8,128)(2,1)}, u32[]{:S(2)}, u32[]{:S(2)}) async-start(bf16[64,7,2048]{2,1,0:T(8,128)(2,1)} %reshape.144), calls=%async_computation | async-start | bytes 4194304 | tf_op jit(solution)/shard_map/all_to_all | solution.py:34
  30.2 3.7 %copy-start.5 = (s32[1,40,8]{1,2,0:T(8,128)S(1)}, s32[1,40,8]{1,2,0:T(8,128)}, u32[]{:S(2)}) copy-start(s32[1,40,8]{1,2,0:T(8,128)} %param.11) | copy-start | bytes 3844
  34.8 45.3 %copy-start.6 = (s32[320]{0:T(512)}, s32[320]{0:T(512)S(1)}, u32[]{:S(2)}) copy-start(s32[320]{0:T(512)S(1)} %eq.89) | copy-start | bytes 3844
  34.8 54.4 %copy-start.1 = (bf16[1,2048,64]{1,2,0:T(8,128)(2,1)S(1)}, bf16[1,2048,64]{1,2,0:T(8,128)(2,1)}, u32[]{:S(2)}) copy-start(bf16[1,2048,64]{1,2,0:T(8,128)(2,1)} %param.14) | copy-start | bytes 786436
  71.9 55.8 %all-to-all-start.1 = ((bf16[64,7,2048]{2,1,0:T(8,128)(2,1)}), bf16[64,7,2048]{2,1,0:T(8,128)(2,1)}, u32[]{:S(2)}, u32[]{:S(2)}) async-start(bf16[64,7,2048]{2,1,0:T(8,128)(2,1)} %reshape.148), calls=%async_computation.1 | async-start | bytes 4194304 | tf_op jit(solution)/shard_map/all_to_all | solution.py:34
  96.1 9.3 %copy-start.2 = (bf16[1,40,2048]{2,1,0:T(8,128)(2,1)S(1)}, bf16[1,40,2048]{2,1,0:T(8,128)(2,1)}, u32[]{:S(2)}) copy-start(bf16[1,40,2048]{2,1,0:T(8,128)(2,1)} %param.8) | copy-start | bytes 491524
  105.5 41.9 %collective-permute-start = (bf16[40,2048]{1,0:T(8,128)(2,1)S(1)}, bf16[40,2048]{1,0:T(8,128)(2,1)}, u32[]{:S(2)}, u32[]{:S(2)}) collective-permute-start(bf16[40,2048]{1,0:T(8,128)(2,1)S(1)} %add_convert_fusion.1), channel_id=1, source_target_pairs={{448,0},{0,64},{64,128},{128,192},{192,256},{256,320},{320,384},{3... | collective-permute-start | bytes 491528 | tf_op jit(solution)/shard_map/ppermute | solution.py:10
  131.5 9.3 %copy-start.3 = (bf16[1,40,2048]{2,1,0:T(8,128)(2,1)S(1)}, bf16[1,40,2048]{2,1,0:T(8,128)(2,1)}, u32[]{:S(2)}) copy-start(bf16[1,40,2048]{2,1,0:T(8,128)(2,1)} %param.9) | copy-start | bytes 491524
  140.8 15.1 %collective-permute-start.1 = (bf16[40,2048]{1,0:T(8,128)(2,1)S(1)}, bf16[40,2048]{1,0:T(8,128)(2,1)S(1)}, u32[]{:S(2)}, u32[]{:S(2)}) collective-permute-start(bf16[40,2048]{1,0:T(8,128)(2,1)S(1)} %add_convert_fusion), channel_id=1, source_target_pairs={{64,0},{128,64},{192,128},{256,192},{320,256},{384,320},{448,384},... | collective-permute-start | bytes 491528 | tf_op jit(solution)/shard_map/ppermute | solution.py:10
where the time goes:
time: 159 us; the launch traced here: 158 us
  waiting for transfers between devices  60.1 us (38%)
  local copies, waits for them, and re-layouts  35.9 us (23%)
  starting transfers between devices  35.8 us (23%)
  other arithmetic  15.5 us (10%)
  matrix products  10.1 us (6%)
    all_to_all x2, waiting for transfers between devices, send_back(): lax.all_to_all(rows, 'expert', split_axis=0, concat_axis=0, tiled=True)  51.5 us
    all_to_all x2, starting transfers between devices, send_back(): lax.all_to_all(rows, 'expert', split_axis=0, concat_axis=0, tiled=True)  21.5 us
    ppermute x2, starting transfers between devices, passed_along(): return lax.ppermute(block, axis, route)  14.3 us
    gather x2, local copies, waits for them, and re-layouts, collect_rows(): flattened[slot_index]  13.5 us
    ppermute x2, waiting for transfers between devices, passed_along(): return lax.ppermute(block, axis, route)  8.52 us
    dot_general x2, matrix products, expert_rows(): expert_out = jnp.dot(hidden, down_w, preferred_element_type=jnp.float32)  7.88 us
    reshape x2, local copies, waits for them, and re-layouts, collect_rows(): flattened = returned.reshape(-1, returned.shape[2])  7.52 us
    reshape x2, local copies, waits for them, and re-layouts, expert_rows(): expert_out.astype(jnp.bfloat16).reshape(experts, capacity, down_w.shape[1])  7.33 us
  transfers between devices with their start and end apart: 4, of which 3 were waited for; matrix products, arithmetic and copies ran while one was open for 31% of the time, Pallas kernels for 0%

commit v1 on v0

v1 whole, which is shorter than its diff:
```python
import functools

import jax
import jax.numpy as jnp
from jax import lax
from jax.experimental import pallas as pl
from jax.experimental.pallas import tpu as pltpu
from jax.sharding import Mesh
from jax.sharding import PartitionSpec as P

TOK = 40
CAP = 7
EXPERTS = 64
NY = 8
ROWS = EXPERTS * CAP
STEP = 512
ORDER = (3, 1, 4, -3, -1, 2, -2, 0)
VMEM = pl.BlockSpec(memory_space=pltpu.VMEM)
F32 = jnp.float32
BF16 = jnp.bfloat16
MIRROR = False


def gate_kernel(tf_ref, tr_ref, rf_ref, rr_ref, router_ref, own_ref, far_ref, m1_ref, m2_ref, m3_ref, table):
    experts = lax.broadcasted_iota(jnp.int32, (EXPERTS, TOK), 0)
    later = lax.broadcasted_iota(jnp.int32, (TOK, TOK), 0) < lax.broadcasted_iota(jnp.int32, (TOK, TOK), 1)
    later = later.astype(F32).astype(BF16)
    shares, ranks = [], []
    for t_ref, r_ref in ((tf_ref, rf_ref), (tr_ref, rr_ref)):
        logits = lax.dot_general(
            router_ref[...], t_ref[...], (((1,), (1,)), ((), ())), preferred_element_type=F32
        )
        named = jnp.zeros((EXPERTS, TOK), F32)
        for k in range(8):
            named = named + (r_ref[k : k + 1, :] == experts).astype(F32)
        raised = jnp.where(named > 0, jnp.exp(logits), 0.0)
        shares.append(raised / jnp.sum(raised, axis=0, keepdims=True))
        rank = jnp.dot(named.astype(BF16), later, preferred_element_type=F32)
        ranks.append(jnp.where(named > 0, rank, -1.0))
    pad = jnp.zeros((EXPERTS, 128 - 2 * TOK), F32)
    table[:EXPERTS] = jnp.concatenate([*shares, pad], axis=1)
    table[EXPERTS:] = jnp.concatenate([*ranks, pad], axis=1)

    def part(ref, at, offset):
        place = lax.rem(lax.axis_index("y").astype(jnp.int32) + offset, NY)
        ref[at : at + 8] = table[pl.ds(place, 8, stride=NY), :]
        ref[at + 8 : at + 16] = table[pl.ds(EXPERTS + place, 8, stride=NY), :]

    part(own_ref, 0, 0)
    part(far_ref, 0, 4)
    for offset, ref in ((1, m1_ref), (2, m2_ref), (3, m3_ref)):
        part(ref, 0, offset)
        part(ref, 16, offset + 4)


def gate_tables(tf, tr, rf, rr, router_t):
    return pl.pallas_call(
        gate_kernel,
        out_shape=[jax.ShapeDtypeStruct((size, 128), F32) for size in (16, 16, 32, 32, 32)],
        in_specs=[VMEM] * 5,
        out_specs=[VMEM] * 5,
        scratch_shapes=[pltpu.VMEM((2 * EXPERTS, 128), F32)],
        cost_estimate=pl.CostEstimate(flops=2 * 80 * 2048 * 64, bytes_accessed=700_000, transcendentals=5120),
    )(tf, tr, rf, rr, router_t)


def combine_kernel(m, own_ref, m1_ref, m2_ref, m3_ref, far_ref, rows_ref, *outs_and_scratch):
    *outs, wide, weights = outs_and_scratch

    @pl.when(pl.program_id(0) == 0)
    def _():
        y = lax.axis_index("y").astype(jnp.int32)
        turn = 1 - 2 * lax.rem(lax.axis_index("section").astype(jnp.int32), 2) if MIRROR else 1
        column = lax.broadcasted_iota(jnp.int32, (1, ROWS), 1)
        zx = sum((column >= NY * CAP * i).astype(jnp.int32) for i in range(1, EXPERTS // NY))
        column = column - NY * CAP * zx
        dest = sum((column >= CAP * i).astype(jnp.int32) for i in range(1, NY))
        slot = (column - CAP * dest).astype(F32)
        tables = jnp.concatenate([own_ref[...], m1_ref[:16], m2_ref[:16], m3_ref[:16], far_ref[...]], axis=0)
        by_token = tables.T[m * TOK : (m + 1) * TOK]
        high = by_token.astype(BF16)
        low = (by_token - high.astype(F32)).astype(BF16)
        behind = (y + NY - dest) & (NY - 1)
        place = lax.broadcasted_iota(jnp.int32, (128, ROWS), 0)
        of_share = (place == behind * 16 + zx).astype(F32).astype(BF16)
        of_rank = (place == behind * 16 + zx + 8).astype(F32).astype(BF16)
        share = jnp.dot(jnp.concatenate([high, low], axis=0), of_share, preferred_element_type=F32)
        mine = jnp.dot(high, of_rank, preferred_element_type=F32) == slot
        share_high = jnp.where(mine, share[:TOK], 0.0)
        share_low = jnp.where(mine, share[TOK:], 0.0)
        for i, k in enumerate(ORDER):
            there = dest == lax.rem(y + NY + turn * k, NY)
            wide[i * TOK : (i + 1) * TOK] = jnp.where(there, share_high, 0.0)
            wide[(NY + i) * TOK : (NY + i + 1) * TOK] = jnp.where(there, share_low, 0.0)
        weights[...] = wide[...].astype(BF16)

    total = jnp.dot(weights[...], rows_ref[...], preferred_element_type=F32)
    summed = (total[: NY * TOK] + total[NY * TOK :]).astype(BF16)
    at = 0
    for out in outs:
        out[...] = summed[at : at + out.shape[0]]
        at += out.shape[0]


def combine(m, tables, rows):
    width = rows.shape[1]
    sizes = (2 * TOK, TOK, 2 * TOK, 3 * TOK)
    whole = lambda shape: pl.BlockSpec(shape, lambda i: (0,) * len(shape))
    return pl.pallas_call(
        functools.partial(combine_kernel, m),
        grid=(width // STEP,),
        out_shape=[jax.ShapeDtypeStruct((size, width), BF16) for size in sizes],
        in_specs=[
            *[whole(table.shape) for table in tables],
            pl.BlockSpec((ROWS, STEP), lambda i: (0, i)),
        ],
        out_specs=[pl.BlockSpec((size, STEP), lambda i: (0, i)) for size in sizes],
        scratch_shapes=[pltpu.VMEM((2 * NY * TOK, ROWS), F32), pltpu.VMEM((2 * NY * TOK, ROWS), BF16)],
        compiler_params=pltpu.CompilerParams(vmem_limit_bytes=32 * 1024 * 1024),
        cost_estimate=pl.CostEstimate(
            flops=4 * NY * TOK * ROWS * width, bytes_accessed=2 * (ROWS + NY * TOK) * width, transcendentals=0
        ),
    )(*tables, rows)


def passed_along(block, axis, distance):
    size = lax.axis_size(axis)
    return lax.ppermute(block, axis, [(i, (i + distance) % size) for i in range(size)])


def onward(block, distance):
    if not MIRROR:
        return passed_along(block, "y", distance)
    ns = lax.axis_size("section")
    route = [
        (s * NY + i, s * NY + (i + (distance if s % 2 == 0 else -distance)) % NY) for s in range(ns) for i in range(NY)
    ]
    return lax.ppermute(block, ("section", "y"), route)


def add(*terms):
    total = terms[0].astype(F32)
    for term in terms[1:]:
        total = total + term.astype(F32)
    return total.astype(BF16)


def shards(tf, tr, rf, rr, hf, hr, router, down):
    tokens = (tf[0], tr[0])
    own, far, *sent = gate_tables(tf[0], tr[0], rf[0].T, rr[0].T, router[0].T)
    hf, *sent = lax.optimization_barrier((hf, *sent))
    near = [passed_along(block, "y", 1 + i) for i, block in enumerate(sent)]
    far = passed_along(jnp.concatenate([far] + [block[16:] for block in near]), "y", 4)
    down_w = down[0, 0]
    arrived = []
    for m, hidden in enumerate((hf, hr)):
        rows = jnp.dot(hidden[0, 0], down_w, preferred_element_type=F32).astype(BF16)
        if m == 1:
            rows, far = lax.optimization_barrier((rows, far))
        back = lax.all_to_all(rows, ("zl", "x"), split_axis=0, concat_axis=0, tiled=True)
        ahead31, ahead4, behind31, kept = combine(m, (own, *near, far), back)
        got_ahead = onward(ahead31, 1)
        got_four = onward(ahead4, 2)
        got_behind = onward(behind31, -1)
        last_ahead = onward(add(kept[:TOK], got_ahead[:TOK], got_four), 2)
        last_behind = onward(add(kept[TOK : 2 * TOK], got_behind[:TOK]), -2)
        layer = add(tokens[m], kept[2 * TOK :], got_ahead[TOK:], got_behind[TOK:], last_ahead, last_behind)
        arrived.append(passed_along(layer, "section", 1 - 2 * m)[None])
    return tuple(arrived)


def solution(mesh):
    fine = Mesh(mesh.devices.reshape(8, 2, 4, NY), ("section", "zl", "x", "y"))
    expert = ("zl", "x", "y")
    row = P("section", expert, None)
    block = P("section", expert, None, None)
    return jax.shard_map(
        shards,
        mesh=fine,
        in_specs=(row, row, row, row, block, block, P("section", None, None), block),
        out_specs=(row, row),
        check_vma=False,
    )
```

time: 159 us -> 121 us (0.76)
  the two profiles are of different devices: /device:TPU:1 before, /device:TPU:82 now
where the time goes in v1:
time: 121 us; the launch traced here: 120 us
  starting transfers between devices  78 us (64%)
  waiting for transfers between devices  15.7 us (13%)
  Pallas kernels  11.1 us (9%)
  matrix products  7.87 us (7%)
  local copies, waits for them, and re-layouts  3.61 us (3%)
  other arithmetic  2.55 us (2%)
    ppermute x16, starting transfers between devices, passed_along(): lax.ppermute(block, axis, [(i, (i + distance) % size) for i in range(size)])  66.4 us
    ppermute x16, waiting for transfers between devices, passed_along(): lax.ppermute(block, axis, [(i, (i + distance) % size) for i in range(size)])  12.9 us
    all_to_all x2, starting transfers between devices, shards(): lax.all_to_all(rows, ('zl', 'x'), split_axis=0, concat_axis=0, tiled=True)  11.6 us
    pallas_call x2, Pallas kernels, combine(): pl.pallas_call(functools.partial(combine_kernel, m), grid=(width // STEP,...  8.75 us
    dot_general x2, matrix products, shards(): jnp.dot(hidden[0, 0], down_w, preferred_element_type=F32).astype(BF16)  7.87 us
    unnamed x24, local copies, waits for them, and re-layouts  3.6 us
    all_to_all x2, waiting for transfers between devices, shards(): lax.all_to_all(rows, ('zl', 'x'), split_axis=0, concat_axis=0, tiled=True)  2.82 us
    convert_element_type x4, other arithmetic, add(): return total.astype(BF16)  2.55 us
  transfers between devices with their start and end apart: 18, of which 6 were waited for; matrix products, arithmetic and copies ran while one was open for 5% of the time, Pallas kernels for 7%

profile of v1, /device:TPU:82, one launch (start us, length us, event | category | flops | bytes accessed | tf_op | source)
XLA Modules:
  0.0 119.7 jit_solution(9309122171763136886)
XLA Ops:
  0.6 0.0 copy-start
  0.6 2.3 %shard_map.95 = (f32[16,128]{1,0:T(8,128)}, f32[16,128]{1,0:T(8,128)}, f32[32,128]{1,0:T(8,128)}, f32[32,128]{1,0:T(8,128)}, f32[32,128]{1,0:T(8,128)}) custom-call(bf16[40,2048]{1,0:T(8,128)(2,1)} %bitcast.36, bf16[40,2048]{1,0:T(8,128)(2,1)} %bitcast.37, s32[8,40]{1,0:T(8,128)} %bitcast.41, s32[8,40]{1,0:T(8,128)} %bitcast.42, bf16[64,2048]{1,0:T(8,128)(2,1)} %bitcast.38), custom_call_target="tpu_custom_call" | custom-call | flops 20971520 | bytes 700000 | tf_op jit(solution)/shard_map/pallas_call | solution.py:57
  3.0 4.0 %fusion.4 = bf16[448,2048]{1,0:T(8,128)(2,1)} fusion(bf16[1,1,768,2048]{3,2,1,0:T(8,128)(2,1)S(1)} %copy-done, bf16[1,1,448,768]{3,2,1,0:T(8,128)(2,1)} %param.12), kind=kOutput, calls=%fused_computation.4 | convolution fusion | flops 1410203648 | bytes 5668864 | tf_op jit(solution)/shard_map/dot_general | solution.py:157
  6.9 5.9 %all-to-all-start = ((bf16[8,56,2048]{2,1,0:T(8,128)(2,1)}), bf16[8,56,2048]{2,1,0:T(8,128)(2,1)}, u32[]{:S(2)}, u32[]{:S(2)}) async-start(bf16[8,56,2048]{2,1,0:T(8,128)(2,1)} %bitcast.34), calls=%async_computation | async-start | bytes 3670016 | tf_op jit(solution)/shard_map/all_to_all | solution.py:160
  12.8 3.5 %collective-permute-start = (f32[32,128]{1,0:T(8,128)S(1)}, f32[32,128]{1,0:T(8,128)S(1)}, u32[]{:S(2)}, u32[]{:S(2)}) collective-permute-start(f32[32,128]{1,0:T(8,128)S(1)} %copy-done.10), channel_id=1, source_target_pairs={{0,1},{1,2},{2,3},{3,4},{4,5},{5,6},{6,7},{7,0},{8,9},{9,10},{10,1... | collective-permute-start | bytes 49160 | tf_op jit(solution)/shard_map/ppermute | solution.py:128
  16.3 4.8 %collective-permute-start.1 = (f32[32,128]{1,0:T(8,128)S(1)}, f32[32,128]{1,0:T(8,128)S(1)}, u32[]{:S(2)}, u32[]{:S(2)}) collective-permute-start(f32[32,128]{1,0:T(8,128)S(1)} %copy-done.9), channel_id=1, source_target_pairs={{0,2},{1,3},{2,4},{3,5},{4,6},{5,7},{6,0},{7,1},{8,10},{9,11},{10,... | collective-permute-start | bytes 49160 | tf_op jit(solution)/shard_map/ppermute | solution.py:128
  21.1 5.4 %collective-permute-start.2 = (f32[32,128]{1,0:T(8,128)S(1)}, f32[32,128]{1,0:T(8,128)S(1)}, u32[]{:S(2)}, u32[]{:S(2)}) collective-permute-start(f32[32,128]{1,0:T(8,128)S(1)} %copy-done.8), channel_id=1, source_target_pairs={{0,3},{1,4},{2,5},{3,6},{4,7},{5,0},{6,1},{7,2},{8,11},{9,12},{10,... | collective-permute-start | bytes 49160 | tf_op jit(solution)/shard_map/ppermute | solution.py:128
  26.5 0.0 collective-permute-done.m1_ref
  26.5 0.0 collective-permute-done.1.m2_ref
  26.6 3.2 %collective-permute-done.2.m3_ref = f32[32,128]{1,0:T(8,128)S(1)} collective-permute-done((f32[32,128]{1,0:T(8,128)S(1)}, f32[32,128]{1,0:T(8,128)S(1)}, u32[]{:S(2)}, u32[]{:S(2)}) %collective-permute-start.2) | collective-permute-done | bytes 16416 | tf_op jit(solution)/shard_map/ppermute | solution.py:128
  29.8 4.8 %collective-permute-start.3 = (f32[64,128]{1,0:T(8,128)S(1)}, f32[64,128]{1,0:T(8,128)S(1)}, u32[]{:S(2)}, u32[]{:S(2)}) collective-permute-start(f32[64,128]{1,0:T(8,128)S(1)} %pad_maximum_fusion), channel_id=1, source_target_pairs={{0,4},{1,5},{2,6},{3,7},{4,0},{5,1},{6,2},{7,3},{8,12},{9,13},{10,... | collective-permute-start | bytes 98312 | tf_op jit(solution)/shard_map/ppermute | solution.py:128
  34.6 3.9 %fusion.7 = bf16[448,2048]{1,0:T(8,128)(2,1)} fusion(bf16[1,1,768,2048]{3,2,1,0:T(8,128)(2,1)S(1)} %copy-done, bf16[1,1,448,768]{3,2,1,0:T(8,128)(2,1)} %param.13), kind=kOutput, calls=%fused_computation.5 | convolution fusion | flops 1410203648 | bytes 5668864 | tf_op jit(solution)/shard_map/dot_general | solution.py:157
  38.5 0.9 collective-permute-done.3.far_ref
  39.5 0.0 all-to-all-done
  39.5 5.7 %all-to-all-start.1 = ((bf16[8,56,2048]{2,1,0:T(8,128)(2,1)}), bf16[8,56,2048]{2,1,0:T(8,128)(2,1)}, u32[]{:S(2)}, u32[]{:S(2)}) async-start(bf16[8,56,2048]{2,1,0:T(8,128)(2,1)} %bitcast.35), calls=%async_computation.1 | async-start | bytes 3670016 | tf_op jit(solution)/shard_map/all_to_all | solution.py:160
  45.2 0.7 copy-done.3
  45.9 4.6 %shard_map.96 = (bf16[80,2048]{1,0:T(8,128)(2,1)}, bf16[40,2048]{1,0:T(8,128)(2,1)}, bf16[80,2048]{1,0:T(8,128)(2,1)S(1)}, bf16[120,2048]{1,0:T(8,128)(2,1)S(1)}) custom-call(f32[16,128]{1,0:T(8,128)S(1)} %copy-done.3, f32[32,128]{1,0:T(8,128)S(1)} %collective-permute-done.m1_ref, f32[32,128]{1,0:T(8,128)S(1)} %collective-permute-done.1.m2_ref, ...), custom_call_target="tpu_custom_call" | custom-call | flops 1174405120 | bytes 3145728 | tf_op jit(solution)/shard_map/pallas_call | solution.py:109
  50.5 0.8 copy-done.1
  51.3 1.9 %collective-permute-start.4 = (bf16[80,2048]{1,0:T(8,128)(2,1)}, bf16[80,2048]{1,0:T(8,128)(2,1)}, u32[]{:S(2)}, u32[]{:S(2)}) collective-permute-start(bf16[80,2048]{1,0:T(8,128)(2,1)} %get-tuple-element.31), channel_id=1, source_target_pairs={{0,1},{1,2},{2,3},{3,4},{4,5},{5,6},{6,7},{7,0},{8,9},{9,10},{10,1... | collective-permute-start | bytes 983048 | tf_op jit(solution)/shard_map/ppermute | solution.py:128
  53.2 3.9 %collective-permute-start.5 = (bf16[80,2048]{1,0:T(8,128)(2,1)S(1)}, bf16[80,2048]{1,0:T(8,128)(2,1)}, u32[]{:S(2)}, u32[]{:S(2)}) collective-permute-start(bf16[80,2048]{1,0:T(8,128)(2,1)S(1)} %get-tuple-element.32), channel_id=1, source_target_pairs={{0,7},{1,0},{2,1},{3,2},{4,3},{5,4},{6,5},{7,6},{8,15},{9,8},{10,9... | collective-permute-start | bytes 983048 | tf_op jit(solution)/shard_map/ppermute | solution.py:128
  57.2 3.9 %collective-permute-start.6 = (bf16[40,2048]{1,0:T(8,128)(2,1)}, bf16[40,2048]{1,0:T(8,128)(2,1)}, u32[]{:S(2)}, u32[]{:S(2)}) collective-permute-start(bf16[40,2048]{1,0:T(8,128)(2,1)} %get-tuple-element.33), channel_id=1, source_target_pairs={{0,2},{1,3},{2,4},{3,5},{4,6},{5,7},{6,0},{7,1},{8,10},{9,11},{10,... | collective-permute-start | bytes 491528 | tf_op jit(solution)/shard_map/ppermute | solution.py:128
  61.1 2.8 %all-to-all-done.1 = bf16[8,56,2048]{2,1,0:T(8,128)(2,1)} async-done(((bf16[8,56,2048]{2,1,0:T(8,128)(2,1)}), bf16[8,56,2048]{2,1,0:T(8,128)(2,1)}, u32[]{:S(2)}, u32[]{:S(2)}) %all-to-all-start.1) | async-done | bytes 1835040 | tf_op jit(solution)/shard_map/all_to_all | solution.py:160
  63.9 0.8 copy-done.4
  64.7 4.1 %shard_map.97 = (bf16[80,2048]{1,0:T(8,128)(2,1)S(1)}, bf16[40,2048]{1,0:T(8,128)(2,1)S(1)}, bf16[80,2048]{1,0:T(8,128)(2,1)S(1)}, bf16[120,2048]{1,0:T(8,128)(2,1)S(1)}) custom-call(f32[16,128]{1,0:T(8,128)S(1)} %copy-done.4, f32[32,128]{1,0:T(8,128)S(1)} %collective-permute-done.m1_ref, f32[32,128]{1,0:T(8,128)S(1)} %collective-permute-done.1.m2_ref, ...), custom_call_target="tpu_custom_call" | custom-call | flops 1174405120 | bytes 3145728 | tf_op jit(solution)/shard_map/pallas_call | solution.py:109
  68.8 4.4 %collective-permute-start.12 = (bf16[40,2048]{1,0:T(8,128)(2,1)S(1)}, bf16[40,2048]{1,0:T(8,128)(2,1)S(1)}, u32[]{:S(2)}, u32[]{:S(2)}) collective-permute-start(bf16[40,2048]{1,0:T(8,128)(2,1)S(1)} %get-tuple-element.39), channel_id=1, source_target_pairs={{0,2},{1,3},{2,4},{3,5},{4,6},{5,7},{6,0},{7,1},{8,10},{9,11},{10,... | collective-permute-start | bytes 491528 | tf_op jit(solution)/shard_map/ppermute | solution.py:128
  73.2 2.8 %collective-permute-start.10 = (bf16[80,2048]{1,0:T(8,128)(2,1)S(1)}, bf16[80,2048]{1,0:T(8,128)(2,1)S(1)}, u32[]{:S(2)}, u32[]{:S(2)}) collective-permute-start(bf16[80,2048]{1,0:T(8,128)(2,1)S(1)} %get-tuple-element.37), channel_id=1, source_target_pairs={{0,1},{1,2},{2,3},{3,4},{4,5},{5,6},{6,7},{7,0},{8,9},{9,10},{10,1... | collective-permute-start | bytes 983048 | tf_op jit(solution)/shard_map/ppermute | solution.py:128
  76.0 0.0 collective-permute-done.6
  76.0 3.0 %collective-permute-start.11 = (bf16[80,2048]{1,0:T(8,128)(2,1)S(1)}, bf16[80,2048]{1,0:T(8,128)(2,1)S(1)}, u32[]{:S(2)}, u32[]{:S(2)}) collective-permute-start(bf16[80,2048]{1,0:T(8,128)(2,1)S(1)} %get-tuple-element.38), channel_id=1, source_target_pairs={{0,7},{1,0},{2,1},{3,2},{4,3},{5,4},{6,5},{7,6},{8,15},{9,8},{10,9... | collective-permute-start | bytes 983048 | tf_op jit(solution)/shard_map/ppermute | solution.py:128
  79.1 0.0 collective-permute-done.4
  79.1 0.0 collective-permute-done.5
  79.1 1.2 add_convert_fusion.5
  80.3 4.2 %collective-permute-start.7 = (bf16[40,2048]{1,0:T(8,128)(2,1)S(1)}, bf16[40,2048]{1,0:T(8,128)(2,1)S(1)}, u32[]{:S(2)}, u32[]{:S(2)}) collective-permute-start(bf16[40,2048]{1,0:T(8,128)(2,1)S(1)} %get-tuple-element.42), channel_id=1, source_target_pairs={{0,2},{1,3},{2,4},{3,5},{4,6},{5,7},{6,0},{7,1},{8,10},{9,11},{10,... | collective-permute-start | bytes 491528 | tf_op jit(solution)/shard_map/ppermute | solution.py:128
  84.4 2.6 %collective-permute-start.8 = (bf16[40,2048]{1,0:T(8,128)(2,1)S(1)}, bf16[40,2048]{1,0:T(8,128)(2,1)S(1)}, u32[]{:S(2)}, u32[]{:S(2)}) collective-permute-start(bf16[40,2048]{1,0:T(8,128)(2,1)S(1)} %get-tuple-element.43), channel_id=1, source_target_pairs={{0,6},{1,7},{2,0},{3,1},{4,2},{5,3},{6,4},{7,5},{8,14},{9,15},{10,... | collective-permute-start | bytes 491528 | tf_op jit(solution)/shard_map/ppermute | solution.py:128
  87.0 1.6 %collective-permute-done.10 = bf16[80,2048]{1,0:T(8,128)(2,1)S(1)} collective-permute-done((bf16[80,2048]{1,0:T(8,128)(2,1)S(1)}, bf16[80,2048]{1,0:T(8,128)(2,1)S(1)}, u32[]{:S(2)}, u32[]{:S(2)}) %collective-permute-start.10) | collective-permute-done | bytes 327712 | tf_op jit(solution)/shard_map/ppermute | solution.py:128
  88.7 0.1 add_convert_fusion.2
  88.8 6.8 %collective-permute-start.13 = (bf16[40,2048]{1,0:T(8,128)(2,1)S(1)}, bf16[40,2048]{1,0:T(8,128)(2,1)S(1)}, u32[]{:S(2)}, u32[]{:S(2)}) collective-permute-start(bf16[40,2048]{1,0:T(8,128)(2,1)S(1)} %get-tuple-element.40), channel_id=1, source_target_pairs={{0,2},{1,3},{2,4},{3,5},{4,6},{5,7},{6,0},{7,1},{8,10},{9,11},{10,... | collective-permute-start | bytes 491528 | tf_op jit(solution)/shard_map/ppermute | solution.py:128
  95.6 1.9 %collective-permute-start.14 = (bf16[40,2048]{1,0:T(8,128)(2,1)S(1)}, bf16[40,2048]{1,0:T(8,128)(2,1)S(1)}, u32[]{:S(2)}, u32[]{:S(2)}) collective-permute-start(bf16[40,2048]{1,0:T(8,128)(2,1)S(1)} %get-tuple-element.41), channel_id=1, source_target_pairs={{0,6},{1,7},{2,0},{3,1},{4,2},{5,3},{6,4},{7,5},{8,14},{9,15},{10,... | collective-permute-start | bytes 491528 | tf_op jit(solution)/shard_map/ppermute | solution.py:128
  97.5 0.0 collective-permute-done.7
  97.5 0.0 collective-permute-done.8
  97.5 1.1 add_convert_fusion.3
  98.7 1.9 %collective-permute-start.9 = (bf16[40,2048]{1,0:T(8,128)(2,1)S(1)}, bf16[40,2048]{1,0:T(8,128)(2,1)S(1)}, u32[]{:S(2)}, u32[]{:S(2)}) collective-permute-start(bf16[40,2048]{1,0:T(8,128)(2,1)S(1)} %add_convert_fusion.3), channel_id=1, source_target_pairs={{0,64},{64,128},{128,192},{192,256},{256,320},{320,384},{384,448},... | collective-permute-start | bytes 491528 | tf_op jit(solution)/shard_map/ppermute | solution.py:128
  100.6 4.3 %collective-permute-done.14 = bf16[40,2048]{1,0:T(8,128)(2,1)S(1)} collective-permute-done((bf16[40,2048]{1,0:T(8,128)(2,1)S(1)}, bf16[40,2048]{1,0:T(8,128)(2,1)S(1)}, u32[]{:S(2)}, u32[]{:S(2)}) %collective-permute-start.14) | collective-permute-done | bytes 163872 | tf_op jit(solution)/shard_map/ppermute | solution.py:128
  104.9 0.1 add_convert_fusion
  105.0 10.5 %collective-permute-start.15 = (bf16[40,2048]{1,0:T(8,128)(2,1)S(1)}, bf16[40,2048]{1,0:T(8,128)(2,1)S(1)}, u32[]{:S(2)}, u32[]{:S(2)}) collective-permute-start(bf16[40,2048]{1,0:T(8,128)(2,1)S(1)} %add_convert_fusion), channel_id=1, source_target_pairs={{0,448},{64,0},{128,64},{192,128},{256,192},{320,256},{384,320},{4... | collective-permute-start | bytes 491528 | tf_op jit(solution)/shard_map/ppermute | solution.py:128
  115.6 0.0 collective-permute-done.9
  115.6 2.8 %collective-permute-done.15 = bf16[40,2048]{1,0:T(8,128)(2,1)S(1)} collective-permute-done((bf16[40,2048]{1,0:T(8,128)(2,1)S(1)}, bf16[40,2048]{1,0:T(8,128)(2,1)S(1)}, u32[]{:S(2)}, u32[]{:S(2)}) %collective-permute-start.15) | collective-permute-done | bytes 163872 | tf_op jit(solution)/shard_map/ppermute | solution.py:128
  118.4 0.7 copy.12
  119.1 0.7 copy.13
  (25 shorter events, 0.1 us)
Async XLA Ops:
  0.6 2.3 %copy-start = (bf16[1,1,768,2048]{3,2,1,0:T(8,128)(2,1)S(1)}, bf16[1,1,768,2048]{3,2,1,0:T(8,128)(2,1)}, u32[]{:S(2)}) copy-start(bf16[1,1,768,2048]{3,2,1,0:T(8,128)(2,1)} %param.15) | copy-start | bytes 9437188
  6.9 5.9 %copy-start.10 = (f32[32,128]{1,0:T(8,128)S(1)}, f32[32,128]{1,0:T(8,128)}, u32[]{:S(2)}) copy-start(f32[32,128]{1,0:T(8,128)} %get-tuple-element.25) | copy-start | bytes 49156
  6.9 9.4 %copy-start.9 = (f32[32,128]{1,0:T(8,128)S(1)}, f32[32,128]{1,0:T(8,128)}, u32[]{:S(2)}) copy-start(f32[32,128]{1,0:T(8,128)} %get-tuple-element.26) | copy-start | bytes 49156
  6.9 14.2 %copy-start.8 = (f32[32,128]{1,0:T(8,128)S(1)}, f32[32,128]{1,0:T(8,128)}, u32[]{:S(2)}) copy-start(f32[32,128]{1,0:T(8,128)} %get-tuple-element.27) | copy-start | bytes 49156
  6.9 22.8 %copy-start.7 = (f32[16,128]{1,0:T(8,128)S(1)}, f32[16,128]{1,0:T(8,128)}, u32[]{:S(2)}) copy-start(f32[16,128]{1,0:T(8,128)} %get-tuple-element.28) | copy-start | bytes 24580
  6.9 32.6 %all-to-all-start = ((bf16[8,56,2048]{2,1,0:T(8,128)(2,1)}), bf16[8,56,2048]{2,1,0:T(8,128)(2,1)}, u32[]{:S(2)}, u32[]{:S(2)}) async-start(bf16[8,56,2048]{2,1,0:T(8,128)(2,1)} %bitcast.34), calls=%async_computation | async-start | bytes 3670016 | tf_op jit(solution)/shard_map/all_to_all | solution.py:160
  12.8 13.7 %collective-permute-start = (f32[32,128]{1,0:T(8,128)S(1)}, f32[32,128]{1,0:T(8,128)S(1)}, u32[]{:S(2)}, u32[]{:S(2)}) collective-permute-start(f32[32,128]{1,0:T(8,128)S(1)} %copy-done.10), channel_id=1, source_target_pairs={{0,1},{1,2},{2,3},{3,4},{4,5},{5,6},{6,7},{7,0},{8,9},{9,10},{10,1... | collective-permute-start | bytes 49160 | tf_op jit(solution)/shard_map/ppermute | solution.py:128
  16.3 10.2 %collective-permute-start.1 = (f32[32,128]{1,0:T(8,128)S(1)}, f32[32,128]{1,0:T(8,128)S(1)}, u32[]{:S(2)}, u32[]{:S(2)}) collective-permute-start(f32[32,128]{1,0:T(8,128)S(1)} %copy-done.9), channel_id=1, source_target_pairs={{0,2},{1,3},{2,4},{3,5},{4,6},{5,7},{6,0},{7,1},{8,10},{9,11},{10,... | collective-permute-start | bytes 49160 | tf_op jit(solution)/shard_map/ppermute | solution.py:128
  21.1 8.6 %collective-permute-start.2 = (f32[32,128]{1,0:T(8,128)S(1)}, f32[32,128]{1,0:T(8,128)S(1)}, u32[]{:S(2)}, u32[]{:S(2)}) collective-permute-start(f32[32,128]{1,0:T(8,128)S(1)} %copy-done.8), channel_id=1, source_target_pairs={{0,3},{1,4},{2,5},{3,6},{4,7},{5,0},{6,1},{7,2},{8,11},{9,12},{10,... | collective-permute-start | bytes 49160 | tf_op jit(solution)/shard_map/ppermute | solution.py:128
  29.8 9.7 %collective-permute-start.3 = (f32[64,128]{1,0:T(8,128)S(1)}, f32[64,128]{1,0:T(8,128)S(1)}, u32[]{:S(2)}, u32[]{:S(2)}) collective-permute-start(f32[64,128]{1,0:T(8,128)S(1)} %pad_maximum_fusion), channel_id=1, source_target_pairs={{0,4},{1,5},{2,6},{3,7},{4,0},{5,1},{6,2},{7,3},{8,12},{9,13},{10,... | collective-permute-start | bytes 98312 | tf_op jit(solution)/shard_map/ppermute | solution.py:128
  39.5 24.4 %all-to-all-start.1 = ((bf16[8,56,2048]{2,1,0:T(8,128)(2,1)}), bf16[8,56,2048]{2,1,0:T(8,128)(2,1)}, u32[]{:S(2)}, u32[]{:S(2)}) async-start(bf16[8,56,2048]{2,1,0:T(8,128)(2,1)} %bitcast.35), calls=%async_computation.1 | async-start | bytes 3670016 | tf_op jit(solution)/shard_map/all_to_all | solution.py:160
  45.2 0.7 copy-start.3
  50.5 0.8 copy-start.1
  51.3 27.8 %collective-permute-start.4 = (bf16[80,2048]{1,0:T(8,128)(2,1)}, bf16[80,2048]{1,0:T(8,128)(2,1)}, u32[]{:S(2)}, u32[]{:S(2)}) collective-permute-start(bf16[80,2048]{1,0:T(8,128)(2,1)} %get-tuple-element.31), channel_id=1, source_target_pairs={{0,1},{1,2},{2,3},{3,4},{4,5},{5,6},{6,7},{7,0},{8,9},{9,10},{10,1... | collective-permute-start | bytes 983048 | tf_op jit(solution)/shard_map/ppermute | solution.py:128
  53.2 25.8 %collective-permute-start.5 = (bf16[80,2048]{1,0:T(8,128)(2,1)S(1)}, bf16[80,2048]{1,0:T(8,128)(2,1)}, u32[]{:S(2)}, u32[]{:S(2)}) collective-permute-start(bf16[80,2048]{1,0:T(8,128)(2,1)S(1)} %get-tuple-element.32), channel_id=1, source_target_pairs={{0,7},{1,0},{2,1},{3,2},{4,3},{5,4},{6,5},{7,6},{8,15},{9,8},{10,9... | collective-permute-start | bytes 983048 | tf_op jit(solution)/shard_map/ppermute | solution.py:128
  57.2 18.9 %collective-permute-start.6 = (bf16[40,2048]{1,0:T(8,128)(2,1)}, bf16[40,2048]{1,0:T(8,128)(2,1)}, u32[]{:S(2)}, u32[]{:S(2)}) collective-permute-start(bf16[40,2048]{1,0:T(8,128)(2,1)} %get-tuple-element.33), channel_id=1, source_target_pairs={{0,2},{1,3},{2,4},{3,5},{4,6},{5,7},{6,0},{7,1},{8,10},{9,11},{10,... | collective-permute-start | bytes 491528 | tf_op jit(solution)/shard_map/ppermute | solution.py:128
  63.9 15.1 %copy-start.2 = (bf16[120,2048]{1,0:T(8,128)(2,1)S(1)}, bf16[120,2048]{1,0:T(8,128)(2,1)}, u32[]{:S(2)}) copy-start(bf16[120,2048]{1,0:T(8,128)(2,1)} %copy-done.1) | copy-start | bytes 1474564
  63.9 0.8 copy-start.4
  64.7 32.8 %copy-start.5 = (bf16[1,40,2048]{2,1,0:T(8,128)(2,1)S(1)}, bf16[1,40,2048]{2,1,0:T(8,128)(2,1)}, u32[]{:S(2)}) copy-start(bf16[1,40,2048]{2,1,0:T(8,128)(2,1)} %param.8) | copy-start | bytes 491524
  64.7 40.2 %copy-start.6 = (bf16[1,40,2048]{2,1,0:T(8,128)(2,1)S(1)}, bf16[1,40,2048]{2,1,0:T(8,128)(2,1)}, u32[]{:S(2)}) copy-start(bf16[1,40,2048]{2,1,0:T(8,128)(2,1)} %param.9) | copy-start | bytes 491524
  68.8 18.2 %collective-permute-start.12 = (bf16[40,2048]{1,0:T(8,128)(2,1)S(1)}, bf16[40,2048]{1,0:T(8,128)(2,1)S(1)}, u32[]{:S(2)}, u32[]{:S(2)}) collective-permute-start(bf16[40,2048]{1,0:T(8,128)(2,1)S(1)} %get-tuple-element.39), channel_id=1, source_target_pairs={{0,2},{1,3},{2,4},{3,5},{4,6},{5,7},{6,0},{7,1},{8,10},{9,11},{10,... | collective-permute-start | bytes 491528 | tf_op jit(solution)/shard_map/ppermute | solution.py:128
  73.2 15.5 %collective-permute-start.10 = (bf16[80,2048]{1,0:T(8,128)(2,1)S(1)}, bf16[80,2048]{1,0:T(8,128)(2,1)S(1)}, u32[]{:S(2)}, u32[]{:S(2)}) collective-permute-start(bf16[80,2048]{1,0:T(8,128)(2,1)S(1)} %get-tuple-element.37), channel_id=1, source_target_pairs={{0,1},{1,2},{2,3},{3,4},{4,5},{5,6},{6,7},{7,0},{8,9},{9,10},{10,1... | collective-permute-start | bytes 983048 | tf_op jit(solution)/shard_map/ppermute | solution.py:128
  76.0 12.6 %collective-permute-start.11 = (bf16[80,2048]{1,0:T(8,128)(2,1)S(1)}, bf16[80,2048]{1,0:T(8,128)(2,1)S(1)}, u32[]{:S(2)}, u32[]{:S(2)}) collective-permute-start(bf16[80,2048]{1,0:T(8,128)(2,1)S(1)} %get-tuple-element.38), channel_id=1, source_target_pairs={{0,7},{1,0},{2,1},{3,2},{4,3},{5,4},{6,5},{7,6},{8,15},{9,8},{10,9... | collective-permute-start | bytes 983048 | tf_op jit(solution)/shard_map/ppermute | solution.py:128
  80.3 17.2 %collective-permute-start.7 = (bf16[40,2048]{1,0:T(8,128)(2,1)S(1)}, bf16[40,2048]{1,0:T(8,128)(2,1)S(1)}, u32[]{:S(2)}, u32[]{:S(2)}) collective-permute-start(bf16[40,2048]{1,0:T(8,128)(2,1)S(1)} %get-tuple-element.42), channel_id=1, source_target_pairs={{0,2},{1,3},{2,4},{3,5},{4,6},{5,7},{6,0},{7,1},{8,10},{9,11},{10,... | collective-permute-start | bytes 491528 | tf_op jit(solution)/shard_map/ppermute | solution.py:128
  84.4 13.1 %collective-permute-start.8 = (bf16[40,2048]{1,0:T(8,128)(2,1)S(1)}, bf16[40,2048]{1,0:T(8,128)(2,1)S(1)}, u32[]{:S(2)}, u32[]{:S(2)}) collective-permute-start(bf16[40,2048]{1,0:T(8,128)(2,1)S(1)} %get-tuple-element.43), channel_id=1, source_target_pairs={{0,6},{1,7},{2,0},{3,1},{4,2},{5,3},{6,4},{7,5},{8,14},{9,15},{10,... | collective-permute-start | bytes 491528 | tf_op jit(solution)/shard_map/ppermute | solution.py:128
  88.8 11.8 %collective-permute-start.13 = (bf16[40,2048]{1,0:T(8,128)(2,1)S(1)}, bf16[40,2048]{1,0:T(8,128)(2,1)S(1)}, u32[]{:S(2)}, u32[]{:S(2)}) collective-permute-start(bf16[40,2048]{1,0:T(8,128)(2,1)S(1)} %get-tuple-element.40), channel_id=1, source_target_pairs={{0,2},{1,3},{2,4},{3,5},{4,6},{5,7},{6,0},{7,1},{8,10},{9,11},{10,... | collective-permute-start | bytes 491528 | tf_op jit(solution)/shard_map/ppermute | solution.py:128
  95.6 9.3 %collective-permute-start.14 = (bf16[40,2048]{1,0:T(8,128)(2,1)S(1)}, bf16[40,2048]{1,0:T(8,128)(2,1)S(1)}, u32[]{:S(2)}, u32[]{:S(2)}) collective-permute-start(bf16[40,2048]{1,0:T(8,128)(2,1)S(1)} %get-tuple-element.41), channel_id=1, source_target_pairs={{0,6},{1,7},{2,0},{3,1},{4,2},{5,3},{6,4},{7,5},{8,14},{9,15},{10,... | collective-permute-start | bytes 491528 | tf_op jit(solution)/shard_map/ppermute | solution.py:128
  98.7 16.9 %collective-permute-start.9 = (bf16[40,2048]{1,0:T(8,128)(2,1)S(1)}, bf16[40,2048]{1,0:T(8,128)(2,1)S(1)}, u32[]{:S(2)}, u32[]{:S(2)}) collective-permute-start(bf16[40,2048]{1,0:T(8,128)(2,1)S(1)} %add_convert_fusion.3), channel_id=1, source_target_pairs={{0,64},{64,128},{128,192},{192,256},{256,320},{320,384},{384,448},... | collective-permute-start | bytes 491528 | tf_op jit(solution)/shard_map/ppermute | solution.py:128
  105.0 13.3 %collective-permute-start.15 = (bf16[40,2048]{1,0:T(8,128)(2,1)S(1)}, bf16[40,2048]{1,0:T(8,128)(2,1)S(1)}, u32[]{:S(2)}, u32[]{:S(2)}) collective-permute-start(bf16[40,2048]{1,0:T(8,128)(2,1)S(1)} %add_convert_fusion), channel_id=1, source_target_pairs={{0,448},{64,0},{128,64},{192,128},{256,192},{320,256},{384,320},{4... | collective-permute-start | bytes 491528 | tf_op jit(solution)/shard_map/ppermute | solution.py:128

commit v2 on v1

--- a/solution.py
+++ b/solution.py
@@ -18,7 +18,6 @@
 VMEM = pl.BlockSpec(memory_space=pltpu.VMEM)
 F32 = jnp.float32
 BF16 = jnp.bfloat16
-MIRROR = False
 
 
 def gate_kernel(tf_ref, tr_ref, rf_ref, rr_ref, router_ref, own_ref, far_ref, m1_ref, m2_ref, m3_ref, table):
@@ -64,19 +63,18 @@
     )(tf, tr, rf, rr, router_t)
 
 
-def combine_kernel(m, own_ref, m1_ref, m2_ref, m3_ref, far_ref, rows_ref, *outs_and_scratch):
+def combine_kernel(m, held_ref, m1_ref, m2_ref, m3_ref, far_ref, rows_ref, *outs_and_scratch):
     *outs, wide, weights = outs_and_scratch
 
     @pl.when(pl.program_id(0) == 0)
     def _():
         y = lax.axis_index("y").astype(jnp.int32)
-        turn = 1 - 2 * lax.rem(lax.axis_index("section").astype(jnp.int32), 2) if MIRROR else 1
         column = lax.broadcasted_iota(jnp.int32, (1, ROWS), 1)
         zx = sum((column >= NY * CAP * i).astype(jnp.int32) for i in range(1, EXPERTS // NY))
         column = column - NY * CAP * zx
         dest = sum((column >= CAP * i).astype(jnp.int32) for i in range(1, NY))
         slot = (column - CAP * dest).astype(F32)
-        tables = jnp.concatenate([own_ref[...], m1_ref[:16], m2_ref[:16], m3_ref[:16], far_ref[...]], axis=0)
+        tables = jnp.concatenate([held_ref[64:], m1_ref[:16], m2_ref[:16], m3_ref[:16], far_ref[:64]], axis=0)
         by_token = tables.T[m * TOK : (m + 1) * TOK]
         high = by_token.astype(BF16)
         low = (by_token - high.astype(F32)).astype(BF16)
@@ -89,7 +87,7 @@
         share_high = jnp.where(mine, share[:TOK], 0.0)
         share_low = jnp.where(mine, share[TOK:], 0.0)
         for i, k in enumerate(ORDER):
-            there = dest == lax.rem(y + NY + turn * k, NY)
+            there = dest == lax.rem(y + NY + k, NY)
             wide[i * TOK : (i + 1) * TOK] = jnp.where(there, share_high, 0.0)
             wide[(NY + i) * TOK : (NY + i + 1) * TOK] = jnp.where(there, share_low, 0.0)
         weights[...] = wide[...].astype(BF16)
@@ -128,13 +126,9 @@
     return lax.ppermute(block, axis, [(i, (i + distance) % size) for i in range(size)])
 
 
-def onward(block, distance):
-    if not MIRROR:
-        return passed_along(block, "y", distance)
+def halfway(block):
     ns = lax.axis_size("section")
-    route = [
-        (s * NY + i, s * NY + (i + (distance if s % 2 == 0 else -distance)) % NY) for s in range(ns) for i in range(NY)
-    ]
+    route = [(s * NY + i, s * NY + (i + (2 if s % 2 == 0 else -2)) % NY) for s in range(ns) for i in range(NY)]
     return lax.ppermute(block, ("section", "y"), route)
 
 
@@ -147,10 +141,12 @@
 
 def shards(tf, tr, rf, rr, hf, hr, router, down):
     tokens = (tf[0], tr[0])
+    up = lax.axis_index("section") % 2 == 0
     own, far, *sent = gate_tables(tf[0], tr[0], rf[0].T, rr[0].T, router[0].T)
     hf, *sent = lax.optimization_barrier((hf, *sent))
     near = [passed_along(block, "y", 1 + i) for i, block in enumerate(sent)]
-    far = passed_along(jnp.concatenate([far] + [block[16:] for block in near]), "y", 4)
+    held = jnp.concatenate([far] + [block[16:] for block in near] + [own])
+    far = passed_along(held, "y", 4)
     down_w = down[0, 0]
     arrived = []
     for m, hidden in enumerate((hf, hr)):
@@ -158,12 +154,14 @@
         if m == 1:
             rows, far = lax.optimization_barrier((rows, far))
         back = lax.all_to_all(rows, ("zl", "x"), split_axis=0, concat_axis=0, tiled=True)
-        ahead31, ahead4, behind31, kept = combine(m, (own, *near, far), back)
-        got_ahead = onward(ahead31, 1)
-        got_four = onward(ahead4, 2)
-        got_behind = onward(behind31, -1)
-        last_ahead = onward(add(kept[:TOK], got_ahead[:TOK], got_four), 2)
-        last_behind = onward(add(kept[TOK : 2 * TOK], got_behind[:TOK]), -2)
+        ahead31, ahead4, behind31, kept = combine(m, (held, *near, far), back)
+        got_ahead = passed_along(ahead31, "y", 1)
+        got_four = halfway(ahead4)
+        got_behind = passed_along(behind31, "y", -1)
+        last_ahead = add(kept[:TOK], got_ahead[:TOK], jnp.where(up, got_four, 0))
+        last_behind = add(kept[TOK : 2 * TOK], got_behind[:TOK], jnp.where(up, 0, got_four))
+        last_ahead = passed_along(last_ahead, "y", 2)
+        last_behind = passed_along(last_behind, "y", -2)
         layer = add(tokens[m], kept[2 * TOK :], got_ahead[TOK:], got_behind[TOK:], last_ahead, last_behind)
         arrived.append(passed_along(layer, "section", 1 - 2 * m)[None])
     return tuple(arrived)

time: 121 us -> 121 us (level)
  the two profiles are of different devices: /device:TPU:82 before, /device:TPU:1 now
where the time goes in v2:
time: 121 us; the launch traced here: 119 us
  starting transfers between devices  79.6 us (66%)
  waiting for transfers between devices  14.8 us (12%)
  Pallas kernels  11.2 us (9%)
  matrix products  7.92 us (7%)
  other arithmetic  2.62 us (2%)
  local copies, waits for them, and re-layouts  2.19 us (2%)
    ppermute x14, starting transfers between devices, passed_along(): lax.ppermute(block, axis, [(i, (i + distance) % size) for i in range(size)])  60.3 us
    all_to_all x2, starting transfers between devices, shards(): lax.all_to_all(rows, ('zl', 'x'), split_axis=0, concat_axis=0, tiled=True)  11.5 us
    ppermute x14, waiting for transfers between devices, passed_along(): lax.ppermute(block, axis, [(i, (i + distance) % size) for i in range(size)])  10.2 us
    pallas_call x2, Pallas kernels, combine(): pl.pallas_call(functools.partial(combine_kernel, m), grid=(width // STEP,...  8.89 us
    dot_general x2, matrix products, shards(): jnp.dot(hidden[0, 0], down_w, preferred_element_type=F32).astype(BF16)  7.92 us
    ppermute x2, starting transfers between devices, halfway(): return lax.ppermute(block, ('section', 'y'), route)  7.8 us
    all_to_all x2, waiting for transfers between devices, shards(): lax.all_to_all(rows, ('zl', 'x'), split_axis=0, concat_axis=0, tiled=True)  4.6 us
    convert_element_type x4, other arithmetic, add(): return total.astype(BF16)  2.62 us
  transfers between devices with their start and end apart: 18, of which 5 were waited for; matrix products, arithmetic and copies ran while one was open for 6% of the time, Pallas kernels for 7%

profile of v2, /device:TPU:1, one launch (start us, length us, event | category | flops | bytes accessed | tf_op | source)
XLA Modules:
  0.0 119.2 jit_solution(12531617909154177359)
XLA Ops:
  0.6 0.0 copy-start
  0.6 2.3 %shard_map.95 = (f32[16,128]{1,0:T(8,128)}, f32[16,128]{1,0:T(8,128)}, f32[32,128]{1,0:T(8,128)}, f32[32,128]{1,0:T(8,128)}, f32[32,128]{1,0:T(8,128)}) custom-call(bf16[40,2048]{1,0:T(8,128)(2,1)} %bitcast.36, bf16[40,2048]{1,0:T(8,128)(2,1)} %bitcast.37, s32[8,40]{1,0:T(8,128)} %bitcast.41, s32[8,40]{1,0:T(8,128)} %bitcast.42, bf16[64,2048]{1,0:T(8,128)(2,1)} %bitcast.38), custom_call_target="tpu_custom_call" | custom-call | flops 20971520 | bytes 700000 | tf_op jit(solution)/shard_map/pallas_call | solution.py:56
  3.0 4.0 %fusion.4 = bf16[448,2048]{1,0:T(8,128)(2,1)} fusion(bf16[1,1,768,2048]{3,2,1,0:T(8,128)(2,1)S(1)} %copy-done, bf16[1,1,448,768]{3,2,1,0:T(8,128)(2,1)} %param.12), kind=kOutput, calls=%fused_computation.4 | convolution fusion | flops 1410203648 | bytes 5668864 | tf_op jit(solution)/shard_map/dot_general | solution.py:153
  6.9 6.8 %all-to-all-start = ((bf16[8,56,2048]{2,1,0:T(8,128)(2,1)}), bf16[8,56,2048]{2,1,0:T(8,128)(2,1)}, u32[]{:S(2)}, u32[]{:S(2)}) async-start(bf16[8,56,2048]{2,1,0:T(8,128)(2,1)} %bitcast.35), calls=%async_computation | async-start | bytes 3670016 | tf_op jit(solution)/shard_map/all_to_all | solution.py:156
  13.8 3.2 %collective-permute-start = (f32[32,128]{1,0:T(8,128)S(1)}, f32[32,128]{1,0:T(8,128)S(1)}, u32[]{:S(2)}, u32[]{:S(2)}) collective-permute-start(f32[32,128]{1,0:T(8,128)S(1)} %copy-done.9), channel_id=1, source_target_pairs={{0,1},{1,2},{2,3},{3,4},{4,5},{5,6},{6,7},{7,0},{8,9},{9,10},{10,1... | collective-permute-start | bytes 49160 | tf_op jit(solution)/shard_map/ppermute | solution.py:126
  17.0 4.2 %collective-permute-start.1 = (f32[32,128]{1,0:T(8,128)S(1)}, f32[32,128]{1,0:T(8,128)S(1)}, u32[]{:S(2)}, u32[]{:S(2)}) collective-permute-start(f32[32,128]{1,0:T(8,128)S(1)} %copy-done.8), channel_id=1, source_target_pairs={{0,2},{1,3},{2,4},{3,5},{4,6},{5,7},{6,0},{7,1},{8,10},{9,11},{10,... | collective-permute-start | bytes 49160 | tf_op jit(solution)/shard_map/ppermute | solution.py:126
  21.2 4.6 %collective-permute-start.2 = (f32[32,128]{1,0:T(8,128)S(1)}, f32[32,128]{1,0:T(8,128)S(1)}, u32[]{:S(2)}, u32[]{:S(2)}) collective-permute-start(f32[32,128]{1,0:T(8,128)S(1)} %copy-done.7), channel_id=1, source_target_pairs={{0,3},{1,4},{2,5},{3,6},{4,7},{5,0},{6,1},{7,2},{8,11},{9,12},{10,... | collective-permute-start | bytes 49160 | tf_op jit(solution)/shard_map/ppermute | solution.py:126
  25.9 0.0 collective-permute-done.m1_ref
  25.9 0.0 collective-permute-done.1.m2_ref
  25.9 3.4 %collective-permute-done.2.m3_ref = f32[32,128]{1,0:T(8,128)S(1)} collective-permute-done((f32[32,128]{1,0:T(8,128)S(1)}, f32[32,128]{1,0:T(8,128)S(1)}, u32[]{:S(2)}, u32[]{:S(2)}) %collective-permute-start.2) | collective-permute-done | bytes 16416 | tf_op jit(solution)/shard_map/ppermute | solution.py:126
  29.3 4.5 %collective-permute-start.3 = (f32[80,128]{1,0:T(8,128)S(1)}, f32[80,128]{1,0:T(8,128)S(1)}, u32[]{:S(2)}, u32[]{:S(2)}) collective-permute-start(f32[80,128]{1,0:T(8,128)S(1)} %constant_dynamic-update-slice_fusion.held_ref), channel_id=1, source_target_pairs={{0,4},{1,5},{2,6},{3,7},{4,0},{5,1},{6,2},{7,3},{8,12},{9,13},{10,... | collective-permute-start | bytes 122888 | tf_op jit(solution)/shard_map/ppermute | solution.py:126
  33.9 4.0 %fusion.7 = bf16[448,2048]{1,0:T(8,128)(2,1)} fusion(bf16[1,1,768,2048]{3,2,1,0:T(8,128)(2,1)S(1)} %copy-done, bf16[1,1,448,768]{3,2,1,0:T(8,128)(2,1)} %param.13), kind=kOutput, calls=%fused_computation.5 | convolution fusion | flops 1410203648 | bytes 5668864 | tf_op jit(solution)/shard_map/dot_general | solution.py:153
  37.8 0.2 collective-permute-done.3.far_ref
  38.0 0.0 all-to-all-done
  38.0 4.7 %all-to-all-start.1 = ((bf16[8,56,2048]{2,1,0:T(8,128)(2,1)}), bf16[8,56,2048]{2,1,0:T(8,128)(2,1)}, u32[]{:S(2)}, u32[]{:S(2)}) async-start(bf16[8,56,2048]{2,1,0:T(8,128)(2,1)} %bitcast.34), calls=%async_computation.1 | async-start | bytes 3670016 | tf_op jit(solution)/shard_map/all_to_all | solution.py:156
  42.7 4.7 %shard_map.96 = (bf16[80,2048]{1,0:T(8,128)(2,1)}, bf16[40,2048]{1,0:T(8,128)(2,1)S(1)}, bf16[80,2048]{1,0:T(8,128)(2,1)}, bf16[120,2048]{1,0:T(8,128)(2,1)S(1)}) custom-call(f32[80,128]{1,0:T(8,128)S(1)} %constant_dynamic-update-slice_fusion.held_ref, f32[32,128]{1,0:T(8,128)S(1)} %collective-permute-done.m1_ref, ...), custom_call_target="tpu_custom_call" | custom-call | flops 1174405120 | bytes 3145728 | tf_op jit(solution)/shard_map/pallas_call | solution.py:107
  47.4 0.8 copy-done.1
  48.2 4.3 %collective-permute-start.4 = (bf16[80,2048]{1,0:T(8,128)(2,1)}, bf16[80,2048]{1,0:T(8,128)(2,1)}, u32[]{:S(2)}, u32[]{:S(2)}) collective-permute-start(bf16[80,2048]{1,0:T(8,128)(2,1)} %get-tuple-element.31), channel_id=1, source_target_pairs={{0,1},{1,2},{2,3},{3,4},{4,5},{5,6},{6,7},{7,0},{8,9},{9,10},{10,1... | collective-permute-start | bytes 983048 | tf_op jit(solution)/shard_map/ppermute | solution.py:126
  52.6 2.2 %collective-permute-start.5 = (bf16[80,2048]{1,0:T(8,128)(2,1)}, bf16[80,2048]{1,0:T(8,128)(2,1)}, u32[]{:S(2)}, u32[]{:S(2)}) collective-permute-start(bf16[80,2048]{1,0:T(8,128)(2,1)} %get-tuple-element.32), channel_id=1, source_target_pairs={{0,7},{1,0},{2,1},{3,2},{4,3},{5,4},{6,5},{7,6},{8,15},{9,8},{10,9... | collective-permute-start | bytes 983048 | tf_op jit(solution)/shard_map/ppermute | solution.py:126
  54.7 3.6 %collective-permute-start.6 = (bf16[40,2048]{1,0:T(8,128)(2,1)S(1)}, bf16[40,2048]{1,0:T(8,128)(2,1)}, u32[]{:S(2)}, u32[]{:S(2)}) collective-permute-start(bf16[40,2048]{1,0:T(8,128)(2,1)S(1)} %get-tuple-element.33), channel_id=1, source_target_pairs={{0,2},{1,3},{2,4},{3,5},{4,6},{5,7},{6,0},{7,1},{64,70},{65,71},{6... | collective-permute-start | bytes 491528 | tf_op jit(solution)/shard_map/ppermute | solution.py:132
  58.4 4.6 %all-to-all-done.1 = bf16[8,56,2048]{2,1,0:T(8,128)(2,1)} async-done(((bf16[8,56,2048]{2,1,0:T(8,128)(2,1)}), bf16[8,56,2048]{2,1,0:T(8,128)(2,1)}, u32[]{:S(2)}, u32[]{:S(2)}) %all-to-all-start.1) | async-done | bytes 1835040 | tf_op jit(solution)/shard_map/all_to_all | solution.py:156
  63.0 4.1 %shard_map.97 = (bf16[80,2048]{1,0:T(8,128)(2,1)S(1)}, bf16[40,2048]{1,0:T(8,128)(2,1)S(1)}, bf16[80,2048]{1,0:T(8,128)(2,1)S(1)}, bf16[120,2048]{1,0:T(8,128)(2,1)S(1)}) custom-call(f32[80,128]{1,0:T(8,128)S(1)} %constant_dynamic-update-slice_fusion.held_ref, f32[32,128]{1,0:T(8,128)S(1)} %collective-permute-done.m1_ref, ...), custom_call_target="tpu_custom_call" | custom-call | flops 1174405120 | bytes 3145728 | tf_op jit(solution)/shard_map/pallas_call | solution.py:107
  67.1 4.2 %collective-permute-start.12 = (bf16[40,2048]{1,0:T(8,128)(2,1)S(1)}, bf16[40,2048]{1,0:T(8,128)(2,1)S(1)}, u32[]{:S(2)}, u32[]{:S(2)}) collective-permute-start(bf16[40,2048]{1,0:T(8,128)(2,1)S(1)} %get-tuple-element.39), channel_id=1, source_target_pairs={{0,2},{1,3},{2,4},{3,5},{4,6},{5,7},{6,0},{7,1},{64,70},{65,71},{6... | collective-permute-start | bytes 491528 | tf_op jit(solution)/shard_map/ppermute | solution.py:132
  71.3 3.0 %collective-permute-start.10 = (bf16[80,2048]{1,0:T(8,128)(2,1)S(1)}, bf16[80,2048]{1,0:T(8,128)(2,1)S(1)}, u32[]{:S(2)}, u32[]{:S(2)}) collective-permute-start(bf16[80,2048]{1,0:T(8,128)(2,1)S(1)} %get-tuple-element.37), channel_id=1, source_target_pairs={{0,1},{1,2},{2,3},{3,4},{4,5},{5,6},{6,7},{7,0},{8,9},{9,10},{10,1... | collective-permute-start | bytes 983048 | tf_op jit(solution)/shard_map/ppermute | solution.py:126
  74.3 0.0 collective-permute-done.6
  74.3 3.5 %collective-permute-start.11 = (bf16[80,2048]{1,0:T(8,128)(2,1)S(1)}, bf16[80,2048]{1,0:T(8,128)(2,1)S(1)}, u32[]{:S(2)}, u32[]{:S(2)}) collective-permute-start(bf16[80,2048]{1,0:T(8,128)(2,1)S(1)} %get-tuple-element.38), channel_id=1, source_target_pairs={{0,7},{1,0},{2,1},{3,2},{4,3},{5,4},{6,5},{7,6},{8,15},{9,8},{10,9... | collective-permute-start | bytes 983048 | tf_op jit(solution)/shard_map/ppermute | solution.py:126
  77.9 0.0 collective-permute-done.4
  77.9 0.0 collective-permute-done.5
  77.9 1.2 %add_convert_fusion.5 = (bf16[40,2048]{1,0:T(8,128)(2,1)S(1)}, bf16[40,2048]{1,0:T(8,128)(2,1)S(1)}) fusion(bf16[80,2048]{1,0:T(8,128)(2,1)} %collective-permute-done.4, bf16[40,2048]{1,0:T(8,128)(2,1)} %collective-permute-done.6, bf16[120,2048]{1,0:T(8,128)(2,1)S(1)} %copy-done.2, pred[]{:T(512)S(6)} %eq.5, bf16[80,2048]{1,0:T(8,128)(2,1)} %collective-permute-done.5), kind=kLoop, calls=%fused_computation.13 | loop fusion | flops 1146880 | bytes 1146881 | tf_op jit(solution)/shard_map/convert_element_type | solution.py:139
  79.1 1.9 %collective-permute-start.7 = (bf16[40,2048]{1,0:T(8,128)(2,1)S(1)}, bf16[40,2048]{1,0:T(8,128)(2,1)S(1)}, u32[]{:S(2)}, u32[]{:S(2)}) collective-permute-start(bf16[40,2048]{1,0:T(8,128)(2,1)S(1)} %get-tuple-element.42), channel_id=1, source_target_pairs={{0,2},{1,3},{2,4},{3,5},{4,6},{5,7},{6,0},{7,1},{8,10},{9,11},{10,... | collective-permute-start | bytes 491528 | tf_op jit(solution)/shard_map/ppermute | solution.py:126
  81.0 5.7 %collective-permute-start.8 = (bf16[40,2048]{1,0:T(8,128)(2,1)S(1)}, bf16[40,2048]{1,0:T(8,128)(2,1)S(1)}, u32[]{:S(2)}, u32[]{:S(2)}) collective-permute-start(bf16[40,2048]{1,0:T(8,128)(2,1)S(1)} %get-tuple-element.43), channel_id=1, source_target_pairs={{0,6},{1,7},{2,0},{3,1},{4,2},{5,3},{6,4},{7,5},{8,14},{9,15},{10,... | collective-permute-start | bytes 491528 | tf_op jit(solution)/shard_map/ppermute | solution.py:126
  86.7 0.0 collective-permute-done.12
  86.8 0.0 collective-permute-done.10
  86.8 0.0 collective-permute-done.11
  86.8 0.1 add_convert_fusion.2
  86.9 3.1 %collective-permute-start.13 = (bf16[40,2048]{1,0:T(8,128)(2,1)S(1)}, bf16[40,2048]{1,0:T(8,128)(2,1)S(1)}, u32[]{:S(2)}, u32[]{:S(2)}) collective-permute-start(bf16[40,2048]{1,0:T(8,128)(2,1)S(1)} %get-tuple-element.40), channel_id=1, source_target_pairs={{0,2},{1,3},{2,4},{3,5},{4,6},{5,7},{6,0},{7,1},{8,10},{9,11},{10,... | collective-permute-start | bytes 491528 | tf_op jit(solution)/shard_map/ppermute | solution.py:126
  90.1 4.3 %collective-permute-start.14 = (bf16[40,2048]{1,0:T(8,128)(2,1)S(1)}, bf16[40,2048]{1,0:T(8,128)(2,1)S(1)}, u32[]{:S(2)}, u32[]{:S(2)}) collective-permute-start(bf16[40,2048]{1,0:T(8,128)(2,1)S(1)} %get-tuple-element.41), channel_id=1, source_target_pairs={{0,6},{1,7},{2,0},{3,1},{4,2},{5,3},{6,4},{7,5},{8,14},{9,15},{10,... | collective-permute-start | bytes 491528 | tf_op jit(solution)/shard_map/ppermute | solution.py:126
  94.3 0.0 collective-permute-done.7
  94.3 0.0 collective-permute-done.8
  94.4 1.1 add_convert_fusion.3
  95.5 13.8 %collective-permute-start.9 = (bf16[40,2048]{1,0:T(8,128)(2,1)S(1)}, bf16[40,2048]{1,0:T(8,128)(2,1)S(1)}, u32[]{:S(2)}, u32[]{:S(2)}) collective-permute-start(bf16[40,2048]{1,0:T(8,128)(2,1)S(1)} %add_convert_fusion.3), channel_id=1, source_target_pairs={{0,64},{64,128},{128,192},{192,256},{256,320},{320,384},{384,448},... | collective-permute-start | bytes 491528 | tf_op jit(solution)/shard_map/ppermute | solution.py:126
  109.3 0.0 collective-permute-done.14
  109.3 0.1 add_convert_fusion
  109.4 1.9 %collective-permute-start.15 = (bf16[40,2048]{1,0:T(8,128)(2,1)S(1)}, bf16[40,2048]{1,0:T(8,128)(2,1)S(1)}, u32[]{:S(2)}, u32[]{:S(2)}) collective-permute-start(bf16[40,2048]{1,0:T(8,128)(2,1)S(1)} %add_convert_fusion), channel_id=1, source_target_pairs={{0,448},{64,0},{128,64},{192,128},{256,192},{320,256},{384,320},{4... | collective-permute-start | bytes 491528 | tf_op jit(solution)/shard_map/ppermute | solution.py:126
  111.4 1.1 collective-permute-done.9
  112.5 5.5 %collective-permute-done.15 = bf16[40,2048]{1,0:T(8,128)(2,1)S(1)} collective-permute-done((bf16[40,2048]{1,0:T(8,128)(2,1)S(1)}, bf16[40,2048]{1,0:T(8,128)(2,1)S(1)}, u32[]{:S(2)}, u32[]{:S(2)}) %collective-permute-start.15) | collective-permute-done | bytes 163872 | tf_op jit(solution)/shard_map/ppermute | solution.py:126
  117.9 0.7 copy.16
  118.6 0.7 copy.17
  (24 shorter events, 0.0 us)
Async XLA Ops:
  0.6 2.3 %copy-start = (bf16[1,1,768,2048]{3,2,1,0:T(8,128)(2,1)S(1)}, bf16[1,1,768,2048]{3,2,1,0:T(8,128)(2,1)}, u32[]{:S(2)}) copy-start(bf16[1,1,768,2048]{3,2,1,0:T(8,128)(2,1)} %param.15) | copy-start | bytes 9437188
  6.9 6.8 %copy-start.9 = (f32[32,128]{1,0:T(8,128)S(1)}, f32[32,128]{1,0:T(8,128)}, u32[]{:S(2)}) copy-start(f32[32,128]{1,0:T(8,128)} %get-tuple-element.25) | copy-start | bytes 49156
  6.9 10.0 %copy-start.8 = (f32[32,128]{1,0:T(8,128)S(1)}, f32[32,128]{1,0:T(8,128)}, u32[]{:S(2)}) copy-start(f32[32,128]{1,0:T(8,128)} %get-tuple-element.26) | copy-start | bytes 49156
  6.9 14.3 %copy-start.7 = (f32[32,128]{1,0:T(8,128)S(1)}, f32[32,128]{1,0:T(8,128)}, u32[]{:S(2)}) copy-start(f32[32,128]{1,0:T(8,128)} %get-tuple-element.27) | copy-start | bytes 49156
  6.9 18.9 %copy-start.6 = (f32[16,128]{1,0:T(8,128)S(1)}, f32[16,128]{1,0:T(8,128)}, u32[]{:S(2)}) copy-start(f32[16,128]{1,0:T(8,128)} %get-tuple-element.21) | copy-start | bytes 24580
  6.9 22.4 %copy-start.5 = (f32[16,128]{1,0:T(8,128)S(1)}, f32[16,128]{1,0:T(8,128)}, u32[]{:S(2)}) copy-start(f32[16,128]{1,0:T(8,128)} %get-tuple-element.28) | copy-start | bytes 24580
  6.9 31.1 %all-to-all-start = ((bf16[8,56,2048]{2,1,0:T(8,128)(2,1)}), bf16[8,56,2048]{2,1,0:T(8,128)(2,1)}, u32[]{:S(2)}, u32[]{:S(2)}) async-start(bf16[8,56,2048]{2,1,0:T(8,128)(2,1)} %bitcast.35), calls=%async_computation | async-start | bytes 3670016 | tf_op jit(solution)/shard_map/all_to_all | solution.py:156
  13.8 12.1 %collective-permute-start = (f32[32,128]{1,0:T(8,128)S(1)}, f32[32,128]{1,0:T(8,128)S(1)}, u32[]{:S(2)}, u32[]{:S(2)}) collective-permute-start(f32[32,128]{1,0:T(8,128)S(1)} %copy-done.9), channel_id=1, source_target_pairs={{0,1},{1,2},{2,3},{3,4},{4,5},{5,6},{6,7},{7,0},{8,9},{9,10},{10,1... | collective-permute-start | bytes 49160 | tf_op jit(solution)/shard_map/ppermute | solution.py:126
  17.0 8.9 %collective-permute-start.1 = (f32[32,128]{1,0:T(8,128)S(1)}, f32[32,128]{1,0:T(8,128)S(1)}, u32[]{:S(2)}, u32[]{:S(2)}) collective-permute-start(f32[32,128]{1,0:T(8,128)S(1)} %copy-done.8), channel_id=1, source_target_pairs={{0,2},{1,3},{2,4},{3,5},{4,6},{5,7},{6,0},{7,1},{8,10},{9,11},{10,... | collective-permute-start | bytes 49160 | tf_op jit(solution)/shard_map/ppermute | solution.py:126
  21.2 8.1 %collective-permute-start.2 = (f32[32,128]{1,0:T(8,128)S(1)}, f32[32,128]{1,0:T(8,128)S(1)}, u32[]{:S(2)}, u32[]{:S(2)}) collective-permute-start(f32[32,128]{1,0:T(8,128)S(1)} %copy-done.7), channel_id=1, source_target_pairs={{0,3},{1,4},{2,5},{3,6},{4,7},{5,0},{6,1},{7,2},{8,11},{9,12},{10,... | collective-permute-start | bytes 49160 | tf_op jit(solution)/shard_map/ppermute | solution.py:126
  29.3 8.7 %collective-permute-start.3 = (f32[80,128]{1,0:T(8,128)S(1)}, f32[80,128]{1,0:T(8,128)S(1)}, u32[]{:S(2)}, u32[]{:S(2)}) collective-permute-start(f32[80,128]{1,0:T(8,128)S(1)} %constant_dynamic-update-slice_fusion.held_ref), channel_id=1, source_target_pairs={{0,4},{1,5},{2,6},{3,7},{4,0},{5,1},{6,2},{7,3},{8,12},{9,13},{10,... | collective-permute-start | bytes 122888 | tf_op jit(solution)/shard_map/ppermute | solution.py:126
  38.0 25.0 %all-to-all-start.1 = ((bf16[8,56,2048]{2,1,0:T(8,128)(2,1)}), bf16[8,56,2048]{2,1,0:T(8,128)(2,1)}, u32[]{:S(2)}, u32[]{:S(2)}) async-start(bf16[8,56,2048]{2,1,0:T(8,128)(2,1)} %bitcast.34), calls=%async_computation.1 | async-start | bytes 3670016 | tf_op jit(solution)/shard_map/all_to_all | solution.py:156
  47.4 0.8 copy-start.1
  48.2 29.6 %collective-permute-start.4 = (bf16[80,2048]{1,0:T(8,128)(2,1)}, bf16[80,2048]{1,0:T(8,128)(2,1)}, u32[]{:S(2)}, u32[]{:S(2)}) collective-permute-start(bf16[80,2048]{1,0:T(8,128)(2,1)} %get-tuple-element.31), channel_id=1, source_target_pairs={{0,1},{1,2},{2,3},{3,4},{4,5},{5,6},{6,7},{7,0},{8,9},{9,10},{10,1... | collective-permute-start | bytes 983048 | tf_op jit(solution)/shard_map/ppermute | solution.py:126
  52.6 25.3 %collective-permute-start.5 = (bf16[80,2048]{1,0:T(8,128)(2,1)}, bf16[80,2048]{1,0:T(8,128)(2,1)}, u32[]{:S(2)}, u32[]{:S(2)}) collective-permute-start(bf16[80,2048]{1,0:T(8,128)(2,1)} %get-tuple-element.32), channel_id=1, source_target_pairs={{0,7},{1,0},{2,1},{3,2},{4,3},{5,4},{6,5},{7,6},{8,15},{9,8},{10,9... | collective-permute-start | bytes 983048 | tf_op jit(solution)/shard_map/ppermute | solution.py:126
  54.7 19.6 %collective-permute-start.6 = (bf16[40,2048]{1,0:T(8,128)(2,1)S(1)}, bf16[40,2048]{1,0:T(8,128)(2,1)}, u32[]{:S(2)}, u32[]{:S(2)}) collective-permute-start(bf16[40,2048]{1,0:T(8,128)(2,1)S(1)} %get-tuple-element.33), channel_id=1, source_target_pairs={{0,2},{1,3},{2,4},{3,5},{4,6},{5,7},{6,0},{7,1},{64,70},{65,71},{6... | collective-permute-start | bytes 491528 | tf_op jit(solution)/shard_map/ppermute | solution.py:132
  63.0 14.9 %copy-start.2 = (bf16[120,2048]{1,0:T(8,128)(2,1)S(1)}, bf16[120,2048]{1,0:T(8,128)(2,1)}, u32[]{:S(2)}) copy-start(bf16[120,2048]{1,0:T(8,128)(2,1)} %copy-done.1) | copy-start | bytes 1474564
  63.0 31.4 %copy-start.3 = (bf16[1,40,2048]{2,1,0:T(8,128)(2,1)S(1)}, bf16[1,40,2048]{2,1,0:T(8,128)(2,1)}, u32[]{:S(2)}) copy-start(bf16[1,40,2048]{2,1,0:T(8,128)(2,1)} %param.8) | copy-start | bytes 491524
  63.0 46.3 %copy-start.4 = (bf16[1,40,2048]{2,1,0:T(8,128)(2,1)S(1)}, bf16[1,40,2048]{2,1,0:T(8,128)(2,1)}, u32[]{:S(2)}) copy-start(bf16[1,40,2048]{2,1,0:T(8,128)(2,1)} %param.9) | copy-start | bytes 491524
  67.1 19.6 %collective-permute-start.12 = (bf16[40,2048]{1,0:T(8,128)(2,1)S(1)}, bf16[40,2048]{1,0:T(8,128)(2,1)S(1)}, u32[]{:S(2)}, u32[]{:S(2)}) collective-permute-start(bf16[40,2048]{1,0:T(8,128)(2,1)S(1)} %get-tuple-element.39), channel_id=1, source_target_pairs={{0,2},{1,3},{2,4},{3,5},{4,6},{5,7},{6,0},{7,1},{64,70},{65,71},{6... | collective-permute-start | bytes 491528 | tf_op jit(solution)/shard_map/ppermute | solution.py:132
  71.3 15.4 %collective-permute-start.10 = (bf16[80,2048]{1,0:T(8,128)(2,1)S(1)}, bf16[80,2048]{1,0:T(8,128)(2,1)S(1)}, u32[]{:S(2)}, u32[]{:S(2)}) collective-permute-start(bf16[80,2048]{1,0:T(8,128)(2,1)S(1)} %get-tuple-element.37), channel_id=1, source_target_pairs={{0,1},{1,2},{2,3},{3,4},{4,5},{5,6},{6,7},{7,0},{8,9},{9,10},{10,1... | collective-permute-start | bytes 983048 | tf_op jit(solution)/shard_map/ppermute | solution.py:126
  74.3 12.4 %collective-permute-start.11 = (bf16[80,2048]{1,0:T(8,128)(2,1)S(1)}, bf16[80,2048]{1,0:T(8,128)(2,1)S(1)}, u32[]{:S(2)}, u32[]{:S(2)}) collective-permute-start(bf16[80,2048]{1,0:T(8,128)(2,1)S(1)} %get-tuple-element.38), channel_id=1, source_target_pairs={{0,7},{1,0},{2,1},{3,2},{4,3},{5,4},{6,5},{7,6},{8,15},{9,8},{10,9... | collective-permute-start | bytes 983048 | tf_op jit(solution)/shard_map/ppermute | solution.py:126
  79.1 15.2 %collective-permute-start.7 = (bf16[40,2048]{1,0:T(8,128)(2,1)S(1)}, bf16[40,2048]{1,0:T(8,128)(2,1)S(1)}, u32[]{:S(2)}, u32[]{:S(2)}) collective-permute-start(bf16[40,2048]{1,0:T(8,128)(2,1)S(1)} %get-tuple-element.42), channel_id=1, source_target_pairs={{0,2},{1,3},{2,4},{3,5},{4,6},{5,7},{6,0},{7,1},{8,10},{9,11},{10,... | collective-permute-start | bytes 491528 | tf_op jit(solution)/shard_map/ppermute | solution.py:126
  81.0 13.3 %collective-permute-start.8 = (bf16[40,2048]{1,0:T(8,128)(2,1)S(1)}, bf16[40,2048]{1,0:T(8,128)(2,1)S(1)}, u32[]{:S(2)}, u32[]{:S(2)}) collective-permute-start(bf16[40,2048]{1,0:T(8,128)(2,1)S(1)} %get-tuple-element.43), channel_id=1, source_target_pairs={{0,6},{1,7},{2,0},{3,1},{4,2},{5,3},{6,4},{7,5},{8,14},{9,15},{10,... | collective-permute-start | bytes 491528 | tf_op jit(solution)/shard_map/ppermute | solution.py:126
  86.9 22.3 %collective-permute-start.13 = (bf16[40,2048]{1,0:T(8,128)(2,1)S(1)}, bf16[40,2048]{1,0:T(8,128)(2,1)S(1)}, u32[]{:S(2)}, u32[]{:S(2)}) collective-permute-start(bf16[40,2048]{1,0:T(8,128)(2,1)S(1)} %get-tuple-element.40), channel_id=1, source_target_pairs={{0,2},{1,3},{2,4},{3,5},{4,6},{5,7},{6,0},{7,1},{8,10},{9,11},{10,... | collective-permute-start | bytes 491528 | tf_op jit(solution)/shard_map/ppermute | solution.py:126
  90.1 19.2 %collective-permute-start.14 = (bf16[40,2048]{1,0:T(8,128)(2,1)S(1)}, bf16[40,2048]{1,0:T(8,128)(2,1)S(1)}, u32[]{:S(2)}, u32[]{:S(2)}) collective-permute-start(bf16[40,2048]{1,0:T(8,128)(2,1)S(1)} %get-tuple-element.41), channel_id=1, source_target_pairs={{0,6},{1,7},{2,0},{3,1},{4,2},{5,3},{6,4},{7,5},{8,14},{9,15},{10,... | collective-permute-start | bytes 491528 | tf_op jit(solution)/shard_map/ppermute | solution.py:126
  95.5 17.0 %collective-permute-start.9 = (bf16[40,2048]{1,0:T(8,128)(2,1)S(1)}, bf16[40,2048]{1,0:T(8,128)(2,1)S(1)}, u32[]{:S(2)}, u32[]{:S(2)}) collective-permute-start(bf16[40,2048]{1,0:T(8,128)(2,1)S(1)} %add_convert_fusion.3), channel_id=1, source_target_pairs={{0,64},{64,128},{128,192},{192,256},{256,320},{320,384},{384,448},... | collective-permute-start | bytes 491528 | tf_op jit(solution)/shard_map/ppermute | solution.py:126
  109.4 8.5 %collective-permute-start.15 = (bf16[40,2048]{1,0:T(8,128)(2,1)S(1)}, bf16[40,2048]{1,0:T(8,128)(2,1)S(1)}, u32[]{:S(2)}, u32[]{:S(2)}) collective-permute-start(bf16[40,2048]{1,0:T(8,128)(2,1)S(1)} %add_convert_fusion), channel_id=1, source_target_pairs={{0,448},{64,0},{128,64},{192,128},{256,192},{320,256},{384,320},{4... | collective-permute-start | bytes 491528 | tf_op jit(solution)/shard_map/ppermute | solution.py:126

commit v3 on v2

--- a/solution.py
+++ b/solution.py
@@ -13,7 +13,7 @@
 EXPERTS = 64
 NY = 8
 ROWS = EXPERTS * CAP
-STEP = 512
+STEP = 1024
 ORDER = (3, 1, 4, -3, -1, 2, -2, 0)
 VMEM = pl.BlockSpec(memory_space=pltpu.VMEM)
 F32 = jnp.float32
@@ -64,7 +64,7 @@
 
 
 def combine_kernel(m, held_ref, m1_ref, m2_ref, m3_ref, far_ref, rows_ref, *outs_and_scratch):
-    *outs, wide, weights = outs_and_scratch
+    *outs, weights = outs_and_scratch
 
     @pl.when(pl.program_id(0) == 0)
     def _():
@@ -86,11 +86,9 @@
         mine = jnp.dot(high, of_rank, preferred_element_type=F32) == slot
         share_high = jnp.where(mine, share[:TOK], 0.0)
         share_low = jnp.where(mine, share[TOK:], 0.0)
-        for i, k in enumerate(ORDER):
-            there = dest == lax.rem(y + NY + k, NY)
-            wide[i * TOK : (i + 1) * TOK] = jnp.where(there, share_high, 0.0)
-            wide[(NY + i) * TOK : (NY + i + 1) * TOK] = jnp.where(there, share_low, 0.0)
-        weights[...] = wide[...].astype(BF16)
+        there = [dest == lax.rem(y + NY + k, NY) for k in ORDER]
+        blocks = [jnp.where(at, part, 0.0) for part in (share_high, share_low) for at in there]
+        weights[...] = jnp.concatenate(blocks, axis=0).astype(BF16)
 
     total = jnp.dot(weights[...], rows_ref[...], preferred_element_type=F32)
     summed = (total[: NY * TOK] + total[NY * TOK :]).astype(BF16)
@@ -113,7 +111,7 @@
             pl.BlockSpec((ROWS, STEP), lambda i: (0, i)),
         ],
         out_specs=[pl.BlockSpec((size, STEP), lambda i: (0, i)) for size in sizes],
-        scratch_shapes=[pltpu.VMEM((2 * NY * TOK, ROWS), F32), pltpu.VMEM((2 * NY * TOK, ROWS), BF16)],
+        scratch_shapes=[pltpu.VMEM((2 * NY * TOK, ROWS), BF16)],
         compiler_params=pltpu.CompilerParams(vmem_limit_bytes=32 * 1024 * 1024),
         cost_estimate=pl.CostEstimate(
             flops=4 * NY * TOK * ROWS * width, bytes_accessed=2 * (ROWS + NY * TOK) * width, transcendentals=0

time: 121 us -> 120 us (level)
  Pallas kernels: 11.2 us -> 9.68 us
    pallas_call x2, Pallas kernels: 8.89 us -> 7.37 us  [combine(): pl.pallas_call(functools.partial(combine_kernel, m), grid=(width // STEP,...]
  transfers between devices with their start and end apart: 18 -> 18, of which waited for: 5 -> 5; matrix products, arithmetic and copies ran while one was open for 6% -> 6% of each run, Pallas kernels for 7% -> 6%
where the time goes in v3:
time: 120 us; the launch traced here: 119 us
  starting transfers between devices  79.6 us (66%)
  waiting for transfers between devices  15.6 us (13%)
  Pallas kernels  9.68 us (8%)
  matrix products  7.92 us (7%)
  other arithmetic  2.62 us (2%)
  local copies, waits for them, and re-layouts  2.19 us (2%)
    ppermute x14, starting transfers between devices, passed_along(): lax.ppermute(block, axis, [(i, (i + distance) % size) for i in range(size)])  60.3 us
    all_to_all x2, starting transfers between devices, shards(): lax.all_to_all(rows, ('zl', 'x'), split_axis=0, concat_axis=0, tiled=True)  11.5 us
    ppermute x14, waiting for transfers between devices, passed_along(): lax.ppermute(block, axis, [(i, (i + distance) % size) for i in range(size)])  10.2 us
    dot_general x2, matrix products, shards(): jnp.dot(hidden[0, 0], down_w, preferred_element_type=F32).astype(BF16)  7.92 us
    ppermute x2, starting transfers between devices, halfway(): return lax.ppermute(block, ('section', 'y'), route)  7.81 us
    pallas_call x2, Pallas kernels, combine(): pl.pallas_call(functools.partial(combine_kernel, m), grid=(width // STEP,...  7.37 us
    all_to_all x2, waiting for transfers between devices, shards(): lax.all_to_all(rows, ('zl', 'x'), split_axis=0, concat_axis=0, tiled=True)  5.38 us
    convert_element_type x4, other arithmetic, add(): return total.astype(BF16)  2.62 us
  transfers between devices with their start and end apart: 18, of which 5 were waited for; matrix products, arithmetic and copies ran while one was open for 6% of the time, Pallas kernels for 6%

profile of v3, /device:TPU:1, one launch (start us, length us, event | category | flops | bytes accessed | tf_op | source)
XLA Modules:
  0.0 118.5 jit_solution(17262852086053830147)
XLA Ops:
  0.6 0.0 copy-start
  0.6 2.3 %shard_map.95 = (f32[16,128]{1,0:T(8,128)}, f32[16,128]{1,0:T(8,128)}, f32[32,128]{1,0:T(8,128)}, f32[32,128]{1,0:T(8,128)}, f32[32,128]{1,0:T(8,128)}) custom-call(bf16[40,2048]{1,0:T(8,128)(2,1)} %bitcast.36, bf16[40,2048]{1,0:T(8,128)(2,1)} %bitcast.37, s32[8,40]{1,0:T(8,128)} %bitcast.41, s32[8,40]{1,0:T(8,128)} %bitcast.42, bf16[64,2048]{1,0:T(8,128)(2,1)} %bitcast.38), custom_call_target="tpu_custom_call" | custom-call | flops 20971520 | bytes 700000 | tf_op jit(solution)/shard_map/pallas_call | solution.py:56
  3.0 4.0 %fusion.4 = bf16[448,2048]{1,0:T(8,128)(2,1)} fusion(bf16[1,1,768,2048]{3,2,1,0:T(8,128)(2,1)S(1)} %copy-done, bf16[1,1,448,768]{3,2,1,0:T(8,128)(2,1)} %param.12), kind=kOutput, calls=%fused_computation.4 | convolution fusion | flops 1410203648 | bytes 5668864 | tf_op jit(solution)/shard_map/dot_general | solution.py:151
  6.9 6.8 %all-to-all-start = ((bf16[8,56,2048]{2,1,0:T(8,128)(2,1)}), bf16[8,56,2048]{2,1,0:T(8,128)(2,1)}, u32[]{:S(2)}, u32[]{:S(2)}) async-start(bf16[8,56,2048]{2,1,0:T(8,128)(2,1)} %bitcast.35), calls=%async_computation | async-start | bytes 3670016 | tf_op jit(solution)/shard_map/all_to_all | solution.py:154
  13.8 3.2 %collective-permute-start = (f32[32,128]{1,0:T(8,128)S(1)}, f32[32,128]{1,0:T(8,128)S(1)}, u32[]{:S(2)}, u32[]{:S(2)}) collective-permute-start(f32[32,128]{1,0:T(8,128)S(1)} %copy-done.9), channel_id=1, source_target_pairs={{0,1},{1,2},{2,3},{3,4},{4,5},{5,6},{6,7},{7,0},{8,9},{9,10},{10,1... | collective-permute-start | bytes 49160 | tf_op jit(solution)/shard_map/ppermute | solution.py:124
  17.0 4.2 %collective-permute-start.1 = (f32[32,128]{1,0:T(8,128)S(1)}, f32[32,128]{1,0:T(8,128)S(1)}, u32[]{:S(2)}, u32[]{:S(2)}) collective-permute-start(f32[32,128]{1,0:T(8,128)S(1)} %copy-done.8), channel_id=1, source_target_pairs={{0,2},{1,3},{2,4},{3,5},{4,6},{5,7},{6,0},{7,1},{8,10},{9,11},{10,... | collective-permute-start | bytes 49160 | tf_op jit(solution)/shard_map/ppermute | solution.py:124
  21.2 4.6 %collective-permute-start.2 = (f32[32,128]{1,0:T(8,128)S(1)}, f32[32,128]{1,0:T(8,128)S(1)}, u32[]{:S(2)}, u32[]{:S(2)}) collective-permute-start(f32[32,128]{1,0:T(8,128)S(1)} %copy-done.7), channel_id=1, source_target_pairs={{0,3},{1,4},{2,5},{3,6},{4,7},{5,0},{6,1},{7,2},{8,11},{9,12},{10,... | collective-permute-start | bytes 49160 | tf_op jit(solution)/shard_map/ppermute | solution.py:124
  25.9 0.0 collective-permute-done.m1_ref
  25.9 0.0 collective-permute-done.1.m2_ref
  25.9 3.4 %collective-permute-done.2.m3_ref = f32[32,128]{1,0:T(8,128)S(1)} collective-permute-done((f32[32,128]{1,0:T(8,128)S(1)}, f32[32,128]{1,0:T(8,128)S(1)}, u32[]{:S(2)}, u32[]{:S(2)}) %collective-permute-start.2) | collective-permute-done | bytes 16416 | tf_op jit(solution)/shard_map/ppermute | solution.py:124
  29.3 4.5 %collective-permute-start.3 = (f32[80,128]{1,0:T(8,128)S(1)}, f32[80,128]{1,0:T(8,128)S(1)}, u32[]{:S(2)}, u32[]{:S(2)}) collective-permute-start(f32[80,128]{1,0:T(8,128)S(1)} %constant_dynamic-update-slice_fusion.held_ref), channel_id=1, source_target_pairs={{0,4},{1,5},{2,6},{3,7},{4,0},{5,1},{6,2},{7,3},{8,12},{9,13},{10,... | collective-permute-start | bytes 122888 | tf_op jit(solution)/shard_map/ppermute | solution.py:124
  33.9 4.0 %fusion.7 = bf16[448,2048]{1,0:T(8,128)(2,1)} fusion(bf16[1,1,768,2048]{3,2,1,0:T(8,128)(2,1)S(1)} %copy-done, bf16[1,1,448,768]{3,2,1,0:T(8,128)(2,1)} %param.13), kind=kOutput, calls=%fused_computation.5 | convolution fusion | flops 1410203648 | bytes 5668864 | tf_op jit(solution)/shard_map/dot_general | solution.py:151
  37.8 0.2 collective-permute-done.3.far_ref
  38.0 0.0 all-to-all-done
  38.0 4.7 %all-to-all-start.1 = ((bf16[8,56,2048]{2,1,0:T(8,128)(2,1)}), bf16[8,56,2048]{2,1,0:T(8,128)(2,1)}, u32[]{:S(2)}, u32[]{:S(2)}) async-start(bf16[8,56,2048]{2,1,0:T(8,128)(2,1)} %bitcast.34), calls=%async_computation.1 | async-start | bytes 3670016 | tf_op jit(solution)/shard_map/all_to_all | solution.py:154
  42.7 4.0 %shard_map.96 = (bf16[80,2048]{1,0:T(8,128)(2,1)}, bf16[40,2048]{1,0:T(8,128)(2,1)S(1)}, bf16[80,2048]{1,0:T(8,128)(2,1)}, bf16[120,2048]{1,0:T(8,128)(2,1)S(1)}) custom-call(f32[80,128]{1,0:T(8,128)S(1)} %constant_dynamic-update-slice_fusion.held_ref, f32[32,128]{1,0:T(8,128)S(1)} %collective-permute-done.m1_ref, ...), custom_call_target="tpu_custom_call" | custom-call | flops 1174405120 | bytes 3145728 | tf_op jit(solution)/shard_map/pallas_call | solution.py:105
  46.7 0.8 copy-done.1
  47.5 4.3 %collective-permute-start.4 = (bf16[80,2048]{1,0:T(8,128)(2,1)}, bf16[80,2048]{1,0:T(8,128)(2,1)}, u32[]{:S(2)}, u32[]{:S(2)}) collective-permute-start(bf16[80,2048]{1,0:T(8,128)(2,1)} %get-tuple-element.31), channel_id=1, source_target_pairs={{0,1},{1,2},{2,3},{3,4},{4,5},{5,6},{6,7},{7,0},{8,9},{9,10},{10,1... | collective-permute-start | bytes 983048 | tf_op jit(solution)/shard_map/ppermute | solution.py:124
  51.8 2.2 %collective-permute-start.5 = (bf16[80,2048]{1,0:T(8,128)(2,1)}, bf16[80,2048]{1,0:T(8,128)(2,1)}, u32[]{:S(2)}, u32[]{:S(2)}) collective-permute-start(bf16[80,2048]{1,0:T(8,128)(2,1)} %get-tuple-element.32), channel_id=1, source_target_pairs={{0,7},{1,0},{2,1},{3,2},{4,3},{5,4},{6,5},{7,6},{8,15},{9,8},{10,9... | collective-permute-start | bytes 983048 | tf_op jit(solution)/shard_map/ppermute | solution.py:124
  54.0 3.6 %collective-permute-start.6 = (bf16[40,2048]{1,0:T(8,128)(2,1)S(1)}, bf16[40,2048]{1,0:T(8,128)(2,1)}, u32[]{:S(2)}, u32[]{:S(2)}) collective-permute-start(bf16[40,2048]{1,0:T(8,128)(2,1)S(1)} %get-tuple-element.33), channel_id=1, source_target_pairs={{0,2},{1,3},{2,4},{3,5},{4,6},{5,7},{6,0},{7,1},{64,70},{65,71},{6... | collective-permute-start | bytes 491528 | tf_op jit(solution)/shard_map/ppermute | solution.py:130
  57.6 5.4 %all-to-all-done.1 = bf16[8,56,2048]{2,1,0:T(8,128)(2,1)} async-done(((bf16[8,56,2048]{2,1,0:T(8,128)(2,1)}), bf16[8,56,2048]{2,1,0:T(8,128)(2,1)}, u32[]{:S(2)}, u32[]{:S(2)}) %all-to-all-start.1) | async-done | bytes 1835040 | tf_op jit(solution)/shard_map/all_to_all | solution.py:154
  63.0 3.4 %shard_map.97 = (bf16[80,2048]{1,0:T(8,128)(2,1)S(1)}, bf16[40,2048]{1,0:T(8,128)(2,1)S(1)}, bf16[80,2048]{1,0:T(8,128)(2,1)S(1)}, bf16[120,2048]{1,0:T(8,128)(2,1)S(1)}) custom-call(f32[80,128]{1,0:T(8,128)S(1)} %constant_dynamic-update-slice_fusion.held_ref, f32[32,128]{1,0:T(8,128)S(1)} %collective-permute-done.m1_ref, ...), custom_call_target="tpu_custom_call" | custom-call | flops 1174405120 | bytes 3145728 | tf_op jit(solution)/shard_map/pallas_call | solution.py:105
  66.4 4.2 %collective-permute-start.12 = (bf16[40,2048]{1,0:T(8,128)(2,1)S(1)}, bf16[40,2048]{1,0:T(8,128)(2,1)S(1)}, u32[]{:S(2)}, u32[]{:S(2)}) collective-permute-start(bf16[40,2048]{1,0:T(8,128)(2,1)S(1)} %get-tuple-element.39), channel_id=1, source_target_pairs={{0,2},{1,3},{2,4},{3,5},{4,6},{5,7},{6,0},{7,1},{64,70},{65,71},{6... | collective-permute-start | bytes 491528 | tf_op jit(solution)/shard_map/ppermute | solution.py:130
  70.6 3.0 %collective-permute-start.10 = (bf16[80,2048]{1,0:T(8,128)(2,1)S(1)}, bf16[80,2048]{1,0:T(8,128)(2,1)S(1)}, u32[]{:S(2)}, u32[]{:S(2)}) collective-permute-start(bf16[80,2048]{1,0:T(8,128)(2,1)S(1)} %get-tuple-element.37), channel_id=1, source_target_pairs={{0,1},{1,2},{2,3},{3,4},{4,5},{5,6},{6,7},{7,0},{8,9},{9,10},{10,1... | collective-permute-start | bytes 983048 | tf_op jit(solution)/shard_map/ppermute | solution.py:124
  73.6 0.0 collective-permute-done.6
  73.6 3.5 %collective-permute-start.11 = (bf16[80,2048]{1,0:T(8,128)(2,1)S(1)}, bf16[80,2048]{1,0:T(8,128)(2,1)S(1)}, u32[]{:S(2)}, u32[]{:S(2)}) collective-permute-start(bf16[80,2048]{1,0:T(8,128)(2,1)S(1)} %get-tuple-element.38), channel_id=1, source_target_pairs={{0,7},{1,0},{2,1},{3,2},{4,3},{5,4},{6,5},{7,6},{8,15},{9,8},{10,9... | collective-permute-start | bytes 983048 | tf_op jit(solution)/shard_map/ppermute | solution.py:124
  77.1 0.0 collective-permute-done.4
  77.1 0.0 collective-permute-done.5
  77.1 1.2 %add_convert_fusion.5 = (bf16[40,2048]{1,0:T(8,128)(2,1)S(1)}, bf16[40,2048]{1,0:T(8,128)(2,1)S(1)}) fusion(bf16[80,2048]{1,0:T(8,128)(2,1)} %collective-permute-done.4, bf16[40,2048]{1,0:T(8,128)(2,1)} %collective-permute-done.6, bf16[120,2048]{1,0:T(8,128)(2,1)S(1)} %copy-done.2, pred[]{:T(512)S(6)} %eq.5, bf16[80,2048]{1,0:T(8,128)(2,1)} %collective-permute-done.5), kind=kLoop, calls=%fused_computation.13 | loop fusion | flops 1146880 | bytes 1146881 | tf_op jit(solution)/shard_map/convert_element_type | solution.py:137
  78.4 1.9 %collective-permute-start.7 = (bf16[40,2048]{1,0:T(8,128)(2,1)S(1)}, bf16[40,2048]{1,0:T(8,128)(2,1)S(1)}, u32[]{:S(2)}, u32[]{:S(2)}) collective-permute-start(bf16[40,2048]{1,0:T(8,128)(2,1)S(1)} %get-tuple-element.42), channel_id=1, source_target_pairs={{0,2},{1,3},{2,4},{3,5},{4,6},{5,7},{6,0},{7,1},{8,10},{9,11},{10,... | collective-permute-start | bytes 491528 | tf_op jit(solution)/shard_map/ppermute | solution.py:124
  80.3 5.7 %collective-permute-start.8 = (bf16[40,2048]{1,0:T(8,128)(2,1)S(1)}, bf16[40,2048]{1,0:T(8,128)(2,1)S(1)}, u32[]{:S(2)}, u32[]{:S(2)}) collective-permute-start(bf16[40,2048]{1,0:T(8,128)(2,1)S(1)} %get-tuple-element.43), channel_id=1, source_target_pairs={{0,6},{1,7},{2,0},{3,1},{4,2},{5,3},{6,4},{7,5},{8,14},{9,15},{10,... | collective-permute-start | bytes 491528 | tf_op jit(solution)/shard_map/ppermute | solution.py:124
  86.0 0.0 collective-permute-done.12
  86.0 0.0 collective-permute-done.10
  86.0 0.0 collective-permute-done.11
  86.0 0.1 add_convert_fusion.2
  86.2 3.1 %collective-permute-start.13 = (bf16[40,2048]{1,0:T(8,128)(2,1)S(1)}, bf16[40,2048]{1,0:T(8,128)(2,1)S(1)}, u32[]{:S(2)}, u32[]{:S(2)}) collective-permute-start(bf16[40,2048]{1,0:T(8,128)(2,1)S(1)} %get-tuple-element.40), channel_id=1, source_target_pairs={{0,2},{1,3},{2,4},{3,5},{4,6},{5,7},{6,0},{7,1},{8,10},{9,11},{10,... | collective-permute-start | bytes 491528 | tf_op jit(solution)/shard_map/ppermute | solution.py:124
  89.3 4.3 %collective-permute-start.14 = (bf16[40,2048]{1,0:T(8,128)(2,1)S(1)}, bf16[40,2048]{1,0:T(8,128)(2,1)S(1)}, u32[]{:S(2)}, u32[]{:S(2)}) collective-permute-start(bf16[40,2048]{1,0:T(8,128)(2,1)S(1)} %get-tuple-element.41), channel_id=1, source_target_pairs={{0,6},{1,7},{2,0},{3,1},{4,2},{5,3},{6,4},{7,5},{8,14},{9,15},{10,... | collective-permute-start | bytes 491528 | tf_op jit(solution)/shard_map/ppermute | solution.py:124
  93.6 0.0 collective-permute-done.7
  93.6 0.0 collective-permute-done.8
  93.6 1.1 add_convert_fusion.3
  94.8 13.8 %collective-permute-start.9 = (bf16[40,2048]{1,0:T(8,128)(2,1)S(1)}, bf16[40,2048]{1,0:T(8,128)(2,1)S(1)}, u32[]{:S(2)}, u32[]{:S(2)}) collective-permute-start(bf16[40,2048]{1,0:T(8,128)(2,1)S(1)} %add_convert_fusion.3), channel_id=1, source_target_pairs={{0,64},{64,128},{128,192},{192,256},{256,320},{320,384},{384,448},... | collective-permute-start | bytes 491528 | tf_op jit(solution)/shard_map/ppermute | solution.py:124
  108.5 0.0 collective-permute-done.13
  108.6 0.1 add_convert_fusion
  108.7 1.9 %collective-permute-start.15 = (bf16[40,2048]{1,0:T(8,128)(2,1)S(1)}, bf16[40,2048]{1,0:T(8,128)(2,1)S(1)}, u32[]{:S(2)}, u32[]{:S(2)}) collective-permute-start(bf16[40,2048]{1,0:T(8,128)(2,1)S(1)} %add_convert_fusion), channel_id=1, source_target_pairs={{0,448},{64,0},{128,64},{192,128},{256,192},{320,256},{384,320},{4... | collective-permute-start | bytes 491528 | tf_op jit(solution)/shard_map/ppermute | solution.py:124
  110.6 1.1 collective-permute-done.9
  111.7 5.5 %collective-permute-done.15 = bf16[40,2048]{1,0:T(8,128)(2,1)S(1)} collective-permute-done((bf16[40,2048]{1,0:T(8,128)(2,1)S(1)}, bf16[40,2048]{1,0:T(8,128)(2,1)S(1)}, u32[]{:S(2)}, u32[]{:S(2)}) %collective-permute-start.15) | collective-permute-done | bytes 163872 | tf_op jit(solution)/shard_map/ppermute | solution.py:124
  117.2 0.7 copy.16
  117.9 0.7 copy.17
  (24 shorter events, 0.0 us)
Async XLA Ops:
  0.6 2.3 %copy-start = (bf16[1,1,768,2048]{3,2,1,0:T(8,128)(2,1)S(1)}, bf16[1,1,768,2048]{3,2,1,0:T(8,128)(2,1)}, u32[]{:S(2)}) copy-start(bf16[1,1,768,2048]{3,2,1,0:T(8,128)(2,1)} %param.15) | copy-start | bytes 9437188
  6.9 6.8 %copy-start.9 = (f32[32,128]{1,0:T(8,128)S(1)}, f32[32,128]{1,0:T(8,128)}, u32[]{:S(2)}) copy-start(f32[32,128]{1,0:T(8,128)} %get-tuple-element.25) | copy-start | bytes 49156
  6.9 10.0 %copy-start.8 = (f32[32,128]{1,0:T(8,128)S(1)}, f32[32,128]{1,0:T(8,128)}, u32[]{:S(2)}) copy-start(f32[32,128]{1,0:T(8,128)} %get-tuple-element.26) | copy-start | bytes 49156
  6.9 14.3 %copy-start.7 = (f32[32,128]{1,0:T(8,128)S(1)}, f32[32,128]{1,0:T(8,128)}, u32[]{:S(2)}) copy-start(f32[32,128]{1,0:T(8,128)} %get-tuple-element.27) | copy-start | bytes 49156
  6.9 18.9 %copy-start.6 = (f32[16,128]{1,0:T(8,128)S(1)}, f32[16,128]{1,0:T(8,128)}, u32[]{:S(2)}) copy-start(f32[16,128]{1,0:T(8,128)} %get-tuple-element.21) | copy-start | bytes 24580
  6.9 22.4 %copy-start.5 = (f32[16,128]{1,0:T(8,128)S(1)}, f32[16,128]{1,0:T(8,128)}, u32[]{:S(2)}) copy-start(f32[16,128]{1,0:T(8,128)} %get-tuple-element.28) | copy-start | bytes 24580
  6.9 31.1 %all-to-all-start = ((bf16[8,56,2048]{2,1,0:T(8,128)(2,1)}), bf16[8,56,2048]{2,1,0:T(8,128)(2,1)}, u32[]{:S(2)}, u32[]{:S(2)}) async-start(bf16[8,56,2048]{2,1,0:T(8,128)(2,1)} %bitcast.35), calls=%async_computation | async-start | bytes 3670016 | tf_op jit(solution)/shard_map/all_to_all | solution.py:154
  13.8 12.1 %collective-permute-start = (f32[32,128]{1,0:T(8,128)S(1)}, f32[32,128]{1,0:T(8,128)S(1)}, u32[]{:S(2)}, u32[]{:S(2)}) collective-permute-start(f32[32,128]{1,0:T(8,128)S(1)} %copy-done.9), channel_id=1, source_target_pairs={{0,1},{1,2},{2,3},{3,4},{4,5},{5,6},{6,7},{7,0},{8,9},{9,10},{10,1... | collective-permute-start | bytes 49160 | tf_op jit(solution)/shard_map/ppermute | solution.py:124
  17.0 8.9 %collective-permute-start.1 = (f32[32,128]{1,0:T(8,128)S(1)}, f32[32,128]{1,0:T(8,128)S(1)}, u32[]{:S(2)}, u32[]{:S(2)}) collective-permute-start(f32[32,128]{1,0:T(8,128)S(1)} %copy-done.8), channel_id=1, source_target_pairs={{0,2},{1,3},{2,4},{3,5},{4,6},{5,7},{6,0},{7,1},{8,10},{9,11},{10,... | collective-permute-start | bytes 49160 | tf_op jit(solution)/shard_map/ppermute | solution.py:124
  21.2 8.1 %collective-permute-start.2 = (f32[32,128]{1,0:T(8,128)S(1)}, f32[32,128]{1,0:T(8,128)S(1)}, u32[]{:S(2)}, u32[]{:S(2)}) collective-permute-start(f32[32,128]{1,0:T(8,128)S(1)} %copy-done.7), channel_id=1, source_target_pairs={{0,3},{1,4},{2,5},{3,6},{4,7},{5,0},{6,1},{7,2},{8,11},{9,12},{10,... | collective-permute-start | bytes 49160 | tf_op jit(solution)/shard_map/ppermute | solution.py:124
  29.3 8.7 %collective-permute-start.3 = (f32[80,128]{1,0:T(8,128)S(1)}, f32[80,128]{1,0:T(8,128)S(1)}, u32[]{:S(2)}, u32[]{:S(2)}) collective-permute-start(f32[80,128]{1,0:T(8,128)S(1)} %constant_dynamic-update-slice_fusion.held_ref), channel_id=1, source_target_pairs={{0,4},{1,5},{2,6},{3,7},{4,0},{5,1},{6,2},{7,3},{8,12},{9,13},{10,... | collective-permute-start | bytes 122888 | tf_op jit(solution)/shard_map/ppermute | solution.py:124
  38.0 25.0 %all-to-all-start.1 = ((bf16[8,56,2048]{2,1,0:T(8,128)(2,1)}), bf16[8,56,2048]{2,1,0:T(8,128)(2,1)}, u32[]{:S(2)}, u32[]{:S(2)}) async-start(bf16[8,56,2048]{2,1,0:T(8,128)(2,1)} %bitcast.34), calls=%async_computation.1 | async-start | bytes 3670016 | tf_op jit(solution)/shard_map/all_to_all | solution.py:154
  46.7 0.8 copy-start.1
  47.5 29.6 %collective-permute-start.4 = (bf16[80,2048]{1,0:T(8,128)(2,1)}, bf16[80,2048]{1,0:T(8,128)(2,1)}, u32[]{:S(2)}, u32[]{:S(2)}) collective-permute-start(bf16[80,2048]{1,0:T(8,128)(2,1)} %get-tuple-element.31), channel_id=1, source_target_pairs={{0,1},{1,2},{2,3},{3,4},{4,5},{5,6},{6,7},{7,0},{8,9},{9,10},{10,1... | collective-permute-start | bytes 983048 | tf_op jit(solution)/shard_map/ppermute | solution.py:124
  51.8 25.3 %collective-permute-start.5 = (bf16[80,2048]{1,0:T(8,128)(2,1)}, bf16[80,2048]{1,0:T(8,128)(2,1)}, u32[]{:S(2)}, u32[]{:S(2)}) collective-permute-start(bf16[80,2048]{1,0:T(8,128)(2,1)} %get-tuple-element.32), channel_id=1, source_target_pairs={{0,7},{1,0},{2,1},{3,2},{4,3},{5,4},{6,5},{7,6},{8,15},{9,8},{10,9... | collective-permute-start | bytes 983048 | tf_op jit(solution)/shard_map/ppermute | solution.py:124
  54.0 19.6 %collective-permute-start.6 = (bf16[40,2048]{1,0:T(8,128)(2,1)S(1)}, bf16[40,2048]{1,0:T(8,128)(2,1)}, u32[]{:S(2)}, u32[]{:S(2)}) collective-permute-start(bf16[40,2048]{1,0:T(8,128)(2,1)S(1)} %get-tuple-element.33), channel_id=1, source_target_pairs={{0,2},{1,3},{2,4},{3,5},{4,6},{5,7},{6,0},{7,1},{64,70},{65,71},{6... | collective-permute-start | bytes 491528 | tf_op jit(solution)/shard_map/ppermute | solution.py:130
  63.0 14.1 %copy-start.2 = (bf16[120,2048]{1,0:T(8,128)(2,1)S(1)}, bf16[120,2048]{1,0:T(8,128)(2,1)}, u32[]{:S(2)}) copy-start(bf16[120,2048]{1,0:T(8,128)(2,1)} %copy-done.1) | copy-start | bytes 1474564
  63.0 30.6 %copy-start.3 = (bf16[1,40,2048]{2,1,0:T(8,128)(2,1)S(1)}, bf16[1,40,2048]{2,1,0:T(8,128)(2,1)}, u32[]{:S(2)}) copy-start(bf16[1,40,2048]{2,1,0:T(8,128)(2,1)} %param.8) | copy-start | bytes 491524
  63.0 45.5 %copy-start.4 = (bf16[1,40,2048]{2,1,0:T(8,128)(2,1)S(1)}, bf16[1,40,2048]{2,1,0:T(8,128)(2,1)}, u32[]{:S(2)}) copy-start(bf16[1,40,2048]{2,1,0:T(8,128)(2,1)} %param.9) | copy-start | bytes 491524
  66.4 19.6 %collective-permute-start.12 = (bf16[40,2048]{1,0:T(8,128)(2,1)S(1)}, bf16[40,2048]{1,0:T(8,128)(2,1)S(1)}, u32[]{:S(2)}, u32[]{:S(2)}) collective-permute-start(bf16[40,2048]{1,0:T(8,128)(2,1)S(1)} %get-tuple-element.39), channel_id=1, source_target_pairs={{0,2},{1,3},{2,4},{3,5},{4,6},{5,7},{6,0},{7,1},{64,70},{65,71},{6... | collective-permute-start | bytes 491528 | tf_op jit(solution)/shard_map/ppermute | solution.py:130
  70.6 15.4 %collective-permute-start.10 = (bf16[80,2048]{1,0:T(8,128)(2,1)S(1)}, bf16[80,2048]{1,0:T(8,128)(2,1)S(1)}, u32[]{:S(2)}, u32[]{:S(2)}) collective-permute-start(bf16[80,2048]{1,0:T(8,128)(2,1)S(1)} %get-tuple-element.37), channel_id=1, source_target_pairs={{0,1},{1,2},{2,3},{3,4},{4,5},{5,6},{6,7},{7,0},{8,9},{9,10},{10,1... | collective-permute-start | bytes 983048 | tf_op jit(solution)/shard_map/ppermute | solution.py:124
  73.6 12.4 %collective-permute-start.11 = (bf16[80,2048]{1,0:T(8,128)(2,1)S(1)}, bf16[80,2048]{1,0:T(8,128)(2,1)S(1)}, u32[]{:S(2)}, u32[]{:S(2)}) collective-permute-start(bf16[80,2048]{1,0:T(8,128)(2,1)S(1)} %get-tuple-element.38), channel_id=1, source_target_pairs={{0,7},{1,0},{2,1},{3,2},{4,3},{5,4},{6,5},{7,6},{8,15},{9,8},{10,9... | collective-permute-start | bytes 983048 | tf_op jit(solution)/shard_map/ppermute | solution.py:124
  78.4 15.2 %collective-permute-start.7 = (bf16[40,2048]{1,0:T(8,128)(2,1)S(1)}, bf16[40,2048]{1,0:T(8,128)(2,1)S(1)}, u32[]{:S(2)}, u32[]{:S(2)}) collective-permute-start(bf16[40,2048]{1,0:T(8,128)(2,1)S(1)} %get-tuple-element.42), channel_id=1, source_target_pairs={{0,2},{1,3},{2,4},{3,5},{4,6},{5,7},{6,0},{7,1},{8,10},{9,11},{10,... | collective-permute-start | bytes 491528 | tf_op jit(solution)/shard_map/ppermute | solution.py:124
  80.3 13.3 %collective-permute-start.8 = (bf16[40,2048]{1,0:T(8,128)(2,1)S(1)}, bf16[40,2048]{1,0:T(8,128)(2,1)S(1)}, u32[]{:S(2)}, u32[]{:S(2)}) collective-permute-start(bf16[40,2048]{1,0:T(8,128)(2,1)S(1)} %get-tuple-element.43), channel_id=1, source_target_pairs={{0,6},{1,7},{2,0},{3,1},{4,2},{5,3},{6,4},{7,5},{8,14},{9,15},{10,... | collective-permute-start | bytes 491528 | tf_op jit(solution)/shard_map/ppermute | solution.py:124
  86.2 22.3 %collective-permute-start.13 = (bf16[40,2048]{1,0:T(8,128)(2,1)S(1)}, bf16[40,2048]{1,0:T(8,128)(2,1)S(1)}, u32[]{:S(2)}, u32[]{:S(2)}) collective-permute-start(bf16[40,2048]{1,0:T(8,128)(2,1)S(1)} %get-tuple-element.40), channel_id=1, source_target_pairs={{0,2},{1,3},{2,4},{3,5},{4,6},{5,7},{6,0},{7,1},{8,10},{9,11},{10,... | collective-permute-start | bytes 491528 | tf_op jit(solution)/shard_map/ppermute | solution.py:124
  89.3 19.2 %collective-permute-start.14 = (bf16[40,2048]{1,0:T(8,128)(2,1)S(1)}, bf16[40,2048]{1,0:T(8,128)(2,1)S(1)}, u32[]{:S(2)}, u32[]{:S(2)}) collective-permute-start(bf16[40,2048]{1,0:T(8,128)(2,1)S(1)} %get-tuple-element.41), channel_id=1, source_target_pairs={{0,6},{1,7},{2,0},{3,1},{4,2},{5,3},{6,4},{7,5},{8,14},{9,15},{10,... | collective-permute-start | bytes 491528 | tf_op jit(solution)/shard_map/ppermute | solution.py:124
  94.8 17.0 %collective-permute-start.9 = (bf16[40,2048]{1,0:T(8,128)(2,1)S(1)}, bf16[40,2048]{1,0:T(8,128)(2,1)S(1)}, u32[]{:S(2)}, u32[]{:S(2)}) collective-permute-start(bf16[40,2048]{1,0:T(8,128)(2,1)S(1)} %add_convert_fusion.3), channel_id=1, source_target_pairs={{0,64},{64,128},{128,192},{192,256},{256,320},{320,384},{384,448},... | collective-permute-start | bytes 491528 | tf_op jit(solution)/shard_map/ppermute | solution.py:124
  108.7 8.5 %collective-permute-start.15 = (bf16[40,2048]{1,0:T(8,128)(2,1)S(1)}, bf16[40,2048]{1,0:T(8,128)(2,1)S(1)}, u32[]{:S(2)}, u32[]{:S(2)}) collective-permute-start(bf16[40,2048]{1,0:T(8,128)(2,1)S(1)} %add_convert_fusion), channel_id=1, source_target_pairs={{0,448},{64,0},{128,64},{192,128},{256,192},{320,256},{384,320},{4... | collective-permute-start | bytes 491528 | tf_op jit(solution)/shard_map/ppermute | solution.py:124

commit v4 on v3

--- a/solution.py
+++ b/solution.py
@@ -13,7 +13,7 @@
 EXPERTS = 64
 NY = 8
 ROWS = EXPERTS * CAP
-STEP = 1024
+STEP = 2048
 ORDER = (3, 1, 4, -3, -1, 2, -2, 0)
 VMEM = pl.BlockSpec(memory_space=pltpu.VMEM)
 F32 = jnp.float32

time: 120 us -> 120 us (level)
  no operation moved by 1% of the time
where the time goes in v4:
time: 120 us; the launch traced here: 119 us
  starting transfers between devices  79.6 us (66%)
  waiting for transfers between devices  15.4 us (13%)
  Pallas kernels  9.78 us (8%)
  matrix products  7.92 us (7%)
  other arithmetic  2.62 us (2%)
  local copies, waits for them, and re-layouts  2.19 us (2%)
    ppermute x14, starting transfers between devices, passed_along(): lax.ppermute(block, axis, [(i, (i + distance) % size) for i in range(size)])  60.3 us
    all_to_all x2, starting transfers between devices, shards(): lax.all_to_all(rows, ('zl', 'x'), split_axis=0, concat_axis=0, tiled=True)  11.5 us
    ppermute x14, waiting for transfers between devices, passed_along(): lax.ppermute(block, axis, [(i, (i + distance) % size) for i in range(size)])  10.2 us
    dot_general x2, matrix products, shards(): jnp.dot(hidden[0, 0], down_w, preferred_element_type=F32).astype(BF16)  7.92 us
    ppermute x2, starting transfers between devices, halfway(): return lax.ppermute(block, ('section', 'y'), route)  7.81 us
    pallas_call x2, Pallas kernels, combine(): pl.pallas_call(functools.partial(combine_kernel, m), grid=(width // STEP,...  7.47 us
    all_to_all x2, waiting for transfers between devices, shards(): lax.all_to_all(rows, ('zl', 'x'), split_axis=0, concat_axis=0, tiled=True)  5.26 us
    convert_element_type x4, other arithmetic, add(): return total.astype(BF16)  2.62 us
  transfers between devices with their start and end apart: 18, of which 5 were waited for; matrix products, arithmetic and copies ran while one was open for 6% of the time, Pallas kernels for 6%

profile of v4, /device:TPU:1, one launch (start us, length us, event | category | flops | bytes accessed | tf_op | source)
XLA Modules:
  0.0 118.5 jit_solution(17092925255819194106)
XLA Ops:
  0.6 0.0 copy-start
  0.6 2.3 %shard_map.95 = (f32[16,128]{1,0:T(8,128)}, f32[16,128]{1,0:T(8,128)}, f32[32,128]{1,0:T(8,128)}, f32[32,128]{1,0:T(8,128)}, f32[32,128]{1,0:T(8,128)}) custom-call(bf16[40,2048]{1,0:T(8,128)(2,1)} %bitcast.36, bf16[40,2048]{1,0:T(8,128)(2,1)} %bitcast.37, s32[8,40]{1,0:T(8,128)} %bitcast.41, s32[8,40]{1,0:T(8,128)} %bitcast.42, bf16[64,2048]{1,0:T(8,128)(2,1)} %bitcast.38), custom_call_target="tpu_custom_call" | custom-call | flops 20971520 | bytes 700000 | tf_op jit(solution)/shard_map/pallas_call | solution.py:56
  3.0 4.0 %fusion.4 = bf16[448,2048]{1,0:T(8,128)(2,1)} fusion(bf16[1,1,768,2048]{3,2,1,0:T(8,128)(2,1)S(1)} %copy-done, bf16[1,1,448,768]{3,2,1,0:T(8,128)(2,1)} %param.12), kind=kOutput, calls=%fused_computation.4 | convolution fusion | flops 1410203648 | bytes 5668864 | tf_op jit(solution)/shard_map/dot_general | solution.py:151
  6.9 6.8 %all-to-all-start = ((bf16[8,56,2048]{2,1,0:T(8,128)(2,1)}), bf16[8,56,2048]{2,1,0:T(8,128)(2,1)}, u32[]{:S(2)}, u32[]{:S(2)}) async-start(bf16[8,56,2048]{2,1,0:T(8,128)(2,1)} %bitcast.35), calls=%async_computation | async-start | bytes 3670016 | tf_op jit(solution)/shard_map/all_to_all | solution.py:154
  13.8 3.2 %collective-permute-start = (f32[32,128]{1,0:T(8,128)S(1)}, f32[32,128]{1,0:T(8,128)S(1)}, u32[]{:S(2)}, u32[]{:S(2)}) collective-permute-start(f32[32,128]{1,0:T(8,128)S(1)} %copy-done.9), channel_id=1, source_target_pairs={{0,1},{1,2},{2,3},{3,4},{4,5},{5,6},{6,7},{7,0},{8,9},{9,10},{10,1... | collective-permute-start | bytes 49160 | tf_op jit(solution)/shard_map/ppermute | solution.py:124
  17.0 4.2 %collective-permute-start.1 = (f32[32,128]{1,0:T(8,128)S(1)}, f32[32,128]{1,0:T(8,128)S(1)}, u32[]{:S(2)}, u32[]{:S(2)}) collective-permute-start(f32[32,128]{1,0:T(8,128)S(1)} %copy-done.8), channel_id=1, source_target_pairs={{0,2},{1,3},{2,4},{3,5},{4,6},{5,7},{6,0},{7,1},{8,10},{9,11},{10,... | collective-permute-start | bytes 49160 | tf_op jit(solution)/shard_map/ppermute | solution.py:124
  21.2 4.6 %collective-permute-start.2 = (f32[32,128]{1,0:T(8,128)S(1)}, f32[32,128]{1,0:T(8,128)S(1)}, u32[]{:S(2)}, u32[]{:S(2)}) collective-permute-start(f32[32,128]{1,0:T(8,128)S(1)} %copy-done.7), channel_id=1, source_target_pairs={{0,3},{1,4},{2,5},{3,6},{4,7},{5,0},{6,1},{7,2},{8,11},{9,12},{10,... | collective-permute-start | bytes 49160 | tf_op jit(solution)/shard_map/ppermute | solution.py:124
  25.9 0.0 collective-permute-done.m1_ref
  25.9 0.0 collective-permute-done.1.m2_ref
  25.9 3.4 %collective-permute-done.2.m3_ref = f32[32,128]{1,0:T(8,128)S(1)} collective-permute-done((f32[32,128]{1,0:T(8,128)S(1)}, f32[32,128]{1,0:T(8,128)S(1)}, u32[]{:S(2)}, u32[]{:S(2)}) %collective-permute-start.2) | collective-permute-done | bytes 16416 | tf_op jit(solution)/shard_map/ppermute | solution.py:124
  29.3 4.5 %collective-permute-start.3 = (f32[80,128]{1,0:T(8,128)S(1)}, f32[80,128]{1,0:T(8,128)S(1)}, u32[]{:S(2)}, u32[]{:S(2)}) collective-permute-start(f32[80,128]{1,0:T(8,128)S(1)} %constant_dynamic-update-slice_fusion.held_ref), channel_id=1, source_target_pairs={{0,4},{1,5},{2,6},{3,7},{4,0},{5,1},{6,2},{7,3},{8,12},{9,13},{10,... | collective-permute-start | bytes 122888 | tf_op jit(solution)/shard_map/ppermute | solution.py:124
  33.9 4.0 %fusion.7 = bf16[448,2048]{1,0:T(8,128)(2,1)} fusion(bf16[1,1,768,2048]{3,2,1,0:T(8,128)(2,1)S(1)} %copy-done, bf16[1,1,448,768]{3,2,1,0:T(8,128)(2,1)} %param.13), kind=kOutput, calls=%fused_computation.5 | convolution fusion | flops 1410203648 | bytes 5668864 | tf_op jit(solution)/shard_map/dot_general | solution.py:151
  37.8 0.2 collective-permute-done.3.far_ref
  38.0 0.0 all-to-all-done
  38.0 4.7 %all-to-all-start.1 = ((bf16[8,56,2048]{2,1,0:T(8,128)(2,1)}), bf16[8,56,2048]{2,1,0:T(8,128)(2,1)}, u32[]{:S(2)}, u32[]{:S(2)}) async-start(bf16[8,56,2048]{2,1,0:T(8,128)(2,1)} %bitcast.34), calls=%async_computation.1 | async-start | bytes 3670016 | tf_op jit(solution)/shard_map/all_to_all | solution.py:154
  42.7 4.1 %shard_map.96 = (bf16[80,2048]{1,0:T(8,128)(2,1)}, bf16[40,2048]{1,0:T(8,128)(2,1)S(1)}, bf16[80,2048]{1,0:T(8,128)(2,1)}, bf16[120,2048]{1,0:T(8,128)(2,1)S(1)}) custom-call(f32[80,128]{1,0:T(8,128)S(1)} %constant_dynamic-update-slice_fusion.held_ref, f32[32,128]{1,0:T(8,128)S(1)} %collective-permute-done.m1_ref, ...), custom_call_target="tpu_custom_call" | custom-call | flops 1174405120 | bytes 3145728 | tf_op jit(solution)/shard_map/pallas_call | solution.py:105
  46.8 0.8 copy-done.1
  47.6 4.3 %collective-permute-start.4 = (bf16[80,2048]{1,0:T(8,128)(2,1)}, bf16[80,2048]{1,0:T(8,128)(2,1)}, u32[]{:S(2)}, u32[]{:S(2)}) collective-permute-start(bf16[80,2048]{1,0:T(8,128)(2,1)} %get-tuple-element.31), channel_id=1, source_target_pairs={{0,1},{1,2},{2,3},{3,4},{4,5},{5,6},{6,7},{7,0},{8,9},{9,10},{10,1... | collective-permute-start | bytes 983048 | tf_op jit(solution)/shard_map/ppermute | solution.py:124
  51.9 2.2 %collective-permute-start.5 = (bf16[80,2048]{1,0:T(8,128)(2,1)}, bf16[80,2048]{1,0:T(8,128)(2,1)}, u32[]{:S(2)}, u32[]{:S(2)}) collective-permute-start(bf16[80,2048]{1,0:T(8,128)(2,1)} %get-tuple-element.32), channel_id=1, source_target_pairs={{0,7},{1,0},{2,1},{3,2},{4,3},{5,4},{6,5},{7,6},{8,15},{9,8},{10,9... | collective-permute-start | bytes 983048 | tf_op jit(solution)/shard_map/ppermute | solution.py:124
  54.1 3.6 %collective-permute-start.6 = (bf16[40,2048]{1,0:T(8,128)(2,1)S(1)}, bf16[40,2048]{1,0:T(8,128)(2,1)}, u32[]{:S(2)}, u32[]{:S(2)}) collective-permute-start(bf16[40,2048]{1,0:T(8,128)(2,1)S(1)} %get-tuple-element.33), channel_id=1, source_target_pairs={{0,2},{1,3},{2,4},{3,5},{4,6},{5,7},{6,0},{7,1},{64,70},{65,71},{6... | collective-permute-start | bytes 491528 | tf_op jit(solution)/shard_map/ppermute | solution.py:130
  57.7 5.3 %all-to-all-done.1 = bf16[8,56,2048]{2,1,0:T(8,128)(2,1)} async-done(((bf16[8,56,2048]{2,1,0:T(8,128)(2,1)}), bf16[8,56,2048]{2,1,0:T(8,128)(2,1)}, u32[]{:S(2)}, u32[]{:S(2)}) %all-to-all-start.1) | async-done | bytes 1835040 | tf_op jit(solution)/shard_map/all_to_all | solution.py:154
  63.0 3.4 %shard_map.97 = (bf16[80,2048]{1,0:T(8,128)(2,1)S(1)}, bf16[40,2048]{1,0:T(8,128)(2,1)S(1)}, bf16[80,2048]{1,0:T(8,128)(2,1)S(1)}, bf16[120,2048]{1,0:T(8,128)(2,1)S(1)}) custom-call(f32[80,128]{1,0:T(8,128)S(1)} %constant_dynamic-update-slice_fusion.held_ref, f32[32,128]{1,0:T(8,128)S(1)} %collective-permute-done.m1_ref, ...), custom_call_target="tpu_custom_call" | custom-call | flops 1174405120 | bytes 3145728 | tf_op jit(solution)/shard_map/pallas_call | solution.py:105
  66.4 4.2 %collective-permute-start.12 = (bf16[40,2048]{1,0:T(8,128)(2,1)S(1)}, bf16[40,2048]{1,0:T(8,128)(2,1)S(1)}, u32[]{:S(2)}, u32[]{:S(2)}) collective-permute-start(bf16[40,2048]{1,0:T(8,128)(2,1)S(1)} %get-tuple-element.39), channel_id=1, source_target_pairs={{0,2},{1,3},{2,4},{3,5},{4,6},{5,7},{6,0},{7,1},{64,70},{65,71},{6... | collective-permute-start | bytes 491528 | tf_op jit(solution)/shard_map/ppermute | solution.py:130
  70.6 3.0 %collective-permute-start.10 = (bf16[80,2048]{1,0:T(8,128)(2,1)S(1)}, bf16[80,2048]{1,0:T(8,128)(2,1)S(1)}, u32[]{:S(2)}, u32[]{:S(2)}) collective-permute-start(bf16[80,2048]{1,0:T(8,128)(2,1)S(1)} %get-tuple-element.37), channel_id=1, source_target_pairs={{0,1},{1,2},{2,3},{3,4},{4,5},{5,6},{6,7},{7,0},{8,9},{9,10},{10,1... | collective-permute-start | bytes 983048 | tf_op jit(solution)/shard_map/ppermute | solution.py:124
  73.6 0.0 collective-permute-done.6
  73.6 3.5 %collective-permute-start.11 = (bf16[80,2048]{1,0:T(8,128)(2,1)S(1)}, bf16[80,2048]{1,0:T(8,128)(2,1)S(1)}, u32[]{:S(2)}, u32[]{:S(2)}) collective-permute-start(bf16[80,2048]{1,0:T(8,128)(2,1)S(1)} %get-tuple-element.38), channel_id=1, source_target_pairs={{0,7},{1,0},{2,1},{3,2},{4,3},{5,4},{6,5},{7,6},{8,15},{9,8},{10,9... | collective-permute-start | bytes 983048 | tf_op jit(solution)/shard_map/ppermute | solution.py:124
  77.1 0.0 collective-permute-done.4
  77.1 0.0 collective-permute-done.5
  77.1 1.2 %add_convert_fusion.5 = (bf16[40,2048]{1,0:T(8,128)(2,1)S(1)}, bf16[40,2048]{1,0:T(8,128)(2,1)S(1)}) fusion(bf16[80,2048]{1,0:T(8,128)(2,1)} %collective-permute-done.4, bf16[40,2048]{1,0:T(8,128)(2,1)} %collective-permute-done.6, bf16[120,2048]{1,0:T(8,128)(2,1)S(1)} %copy-done.2, pred[]{:T(512)S(6)} %eq.5, bf16[80,2048]{1,0:T(8,128)(2,1)} %collective-permute-done.5), kind=kLoop, calls=%fused_computation.13 | loop fusion | flops 1146880 | bytes 1146881 | tf_op jit(solution)/shard_map/convert_element_type | solution.py:137
  78.3 1.9 %collective-permute-start.7 = (bf16[40,2048]{1,0:T(8,128)(2,1)S(1)}, bf16[40,2048]{1,0:T(8,128)(2,1)S(1)}, u32[]{:S(2)}, u32[]{:S(2)}) collective-permute-start(bf16[40,2048]{1,0:T(8,128)(2,1)S(1)} %get-tuple-element.42), channel_id=1, source_target_pairs={{0,2},{1,3},{2,4},{3,5},{4,6},{5,7},{6,0},{7,1},{8,10},{9,11},{10,... | collective-permute-start | bytes 491528 | tf_op jit(solution)/shard_map/ppermute | solution.py:124
  80.3 5.7 %collective-permute-start.8 = (bf16[40,2048]{1,0:T(8,128)(2,1)S(1)}, bf16[40,2048]{1,0:T(8,128)(2,1)S(1)}, u32[]{:S(2)}, u32[]{:S(2)}) collective-permute-start(bf16[40,2048]{1,0:T(8,128)(2,1)S(1)} %get-tuple-element.43), channel_id=1, source_target_pairs={{0,6},{1,7},{2,0},{3,1},{4,2},{5,3},{6,4},{7,5},{8,14},{9,15},{10,... | collective-permute-start | bytes 491528 | tf_op jit(solution)/shard_map/ppermute | solution.py:124
  86.0 0.0 collective-permute-done.12
  86.0 0.0 collective-permute-done.10
  86.0 0.0 collective-permute-done.11
  86.0 0.1 add_convert_fusion.2
  86.2 3.1 %collective-permute-start.13 = (bf16[40,2048]{1,0:T(8,128)(2,1)S(1)}, bf16[40,2048]{1,0:T(8,128)(2,1)S(1)}, u32[]{:S(2)}, u32[]{:S(2)}) collective-permute-start(bf16[40,2048]{1,0:T(8,128)(2,1)S(1)} %get-tuple-element.40), channel_id=1, source_target_pairs={{0,2},{1,3},{2,4},{3,5},{4,6},{5,7},{6,0},{7,1},{8,10},{9,11},{10,... | collective-permute-start | bytes 491528 | tf_op jit(solution)/shard_map/ppermute | solution.py:124
  89.3 4.3 %collective-permute-start.14 = (bf16[40,2048]{1,0:T(8,128)(2,1)S(1)}, bf16[40,2048]{1,0:T(8,128)(2,1)S(1)}, u32[]{:S(2)}, u32[]{:S(2)}) collective-permute-start(bf16[40,2048]{1,0:T(8,128)(2,1)S(1)} %get-tuple-element.41), channel_id=1, source_target_pairs={{0,6},{1,7},{2,0},{3,1},{4,2},{5,3},{6,4},{7,5},{8,14},{9,15},{10,... | collective-permute-start | bytes 491528 | tf_op jit(solution)/shard_map/ppermute | solution.py:124
  93.6 0.0 collective-permute-done.7
  93.6 0.0 collective-permute-done.8
  93.6 1.1 add_convert_fusion.3
  94.7 13.8 %collective-permute-start.9 = (bf16[40,2048]{1,0:T(8,128)(2,1)S(1)}, bf16[40,2048]{1,0:T(8,128)(2,1)S(1)}, u32[]{:S(2)}, u32[]{:S(2)}) collective-permute-start(bf16[40,2048]{1,0:T(8,128)(2,1)S(1)} %add_convert_fusion.3), channel_id=1, source_target_pairs={{0,64},{64,128},{128,192},{192,256},{256,320},{320,384},{384,448},... | collective-permute-start | bytes 491528 | tf_op jit(solution)/shard_map/ppermute | solution.py:124
  108.5 0.0 collective-permute-done.14
  108.6 0.1 add_convert_fusion
  108.7 1.9 %collective-permute-start.15 = (bf16[40,2048]{1,0:T(8,128)(2,1)S(1)}, bf16[40,2048]{1,0:T(8,128)(2,1)S(1)}, u32[]{:S(2)}, u32[]{:S(2)}) collective-permute-start(bf16[40,2048]{1,0:T(8,128)(2,1)S(1)} %add_convert_fusion), channel_id=1, source_target_pairs={{0,448},{64,0},{128,64},{192,128},{256,192},{320,256},{384,320},{4... | collective-permute-start | bytes 491528 | tf_op jit(solution)/shard_map/ppermute | solution.py:124
  110.6 1.1 collective-permute-done.9
  111.7 5.5 %collective-permute-done.15 = bf16[40,2048]{1,0:T(8,128)(2,1)S(1)} collective-permute-done((bf16[40,2048]{1,0:T(8,128)(2,1)S(1)}, bf16[40,2048]{1,0:T(8,128)(2,1)S(1)}, u32[]{:S(2)}, u32[]{:S(2)}) %collective-permute-start.15) | collective-permute-done | bytes 163872 | tf_op jit(solution)/shard_map/ppermute | solution.py:124
  117.2 0.7 copy.16
  117.9 0.7 copy.17
  (24 shorter events, 0.0 us)
Async XLA Ops:
  0.6 2.3 %copy-start = (bf16[1,1,768,2048]{3,2,1,0:T(8,128)(2,1)S(1)}, bf16[1,1,768,2048]{3,2,1,0:T(8,128)(2,1)}, u32[]{:S(2)}) copy-start(bf16[1,1,768,2048]{3,2,1,0:T(8,128)(2,1)} %param.15) | copy-start | bytes 9437188
  6.9 6.8 %copy-start.9 = (f32[32,128]{1,0:T(8,128)S(1)}, f32[32,128]{1,0:T(8,128)}, u32[]{:S(2)}) copy-start(f32[32,128]{1,0:T(8,128)} %get-tuple-element.25) | copy-start | bytes 49156
  6.9 10.0 %copy-start.8 = (f32[32,128]{1,0:T(8,128)S(1)}, f32[32,128]{1,0:T(8,128)}, u32[]{:S(2)}) copy-start(f32[32,128]{1,0:T(8,128)} %get-tuple-element.26) | copy-start | bytes 49156
  6.9 14.3 %copy-start.7 = (f32[32,128]{1,0:T(8,128)S(1)}, f32[32,128]{1,0:T(8,128)}, u32[]{:S(2)}) copy-start(f32[32,128]{1,0:T(8,128)} %get-tuple-element.27) | copy-start | bytes 49156
  6.9 18.9 %copy-start.6 = (f32[16,128]{1,0:T(8,128)S(1)}, f32[16,128]{1,0:T(8,128)}, u32[]{:S(2)}) copy-start(f32[16,128]{1,0:T(8,128)} %get-tuple-element.21) | copy-start | bytes 24580
  6.9 22.4 %copy-start.5 = (f32[16,128]{1,0:T(8,128)S(1)}, f32[16,128]{1,0:T(8,128)}, u32[]{:S(2)}) copy-start(f32[16,128]{1,0:T(8,128)} %get-tuple-element.28) | copy-start | bytes 24580
  6.9 31.1 %all-to-all-start = ((bf16[8,56,2048]{2,1,0:T(8,128)(2,1)}), bf16[8,56,2048]{2,1,0:T(8,128)(2,1)}, u32[]{:S(2)}, u32[]{:S(2)}) async-start(bf16[8,56,2048]{2,1,0:T(8,128)(2,1)} %bitcast.35), calls=%async_computation | async-start | bytes 3670016 | tf_op jit(solution)/shard_map/all_to_all | solution.py:154
  13.8 12.1 %collective-permute-start = (f32[32,128]{1,0:T(8,128)S(1)}, f32[32,128]{1,0:T(8,128)S(1)}, u32[]{:S(2)}, u32[]{:S(2)}) collective-permute-start(f32[32,128]{1,0:T(8,128)S(1)} %copy-done.9), channel_id=1, source_target_pairs={{0,1},{1,2},{2,3},{3,4},{4,5},{5,6},{6,7},{7,0},{8,9},{9,10},{10,1... | collective-permute-start | bytes 49160 | tf_op jit(solution)/shard_map/ppermute | solution.py:124
  17.0 8.9 %collective-permute-start.1 = (f32[32,128]{1,0:T(8,128)S(1)}, f32[32,128]{1,0:T(8,128)S(1)}, u32[]{:S(2)}, u32[]{:S(2)}) collective-permute-start(f32[32,128]{1,0:T(8,128)S(1)} %copy-done.8), channel_id=1, source_target_pairs={{0,2},{1,3},{2,4},{3,5},{4,6},{5,7},{6,0},{7,1},{8,10},{9,11},{10,... | collective-permute-start | bytes 49160 | tf_op jit(solution)/shard_map/ppermute | solution.py:124
  21.2 8.1 %collective-permute-start.2 = (f32[32,128]{1,0:T(8,128)S(1)}, f32[32,128]{1,0:T(8,128)S(1)}, u32[]{:S(2)}, u32[]{:S(2)}) collective-permute-start(f32[32,128]{1,0:T(8,128)S(1)} %copy-done.7), channel_id=1, source_target_pairs={{0,3},{1,4},{2,5},{3,6},{4,7},{5,0},{6,1},{7,2},{8,11},{9,12},{10,... | collective-permute-start | bytes 49160 | tf_op jit(solution)/shard_map/ppermute | solution.py:124
  29.3 8.7 %collective-permute-start.3 = (f32[80,128]{1,0:T(8,128)S(1)}, f32[80,128]{1,0:T(8,128)S(1)}, u32[]{:S(2)}, u32[]{:S(2)}) collective-permute-start(f32[80,128]{1,0:T(8,128)S(1)} %constant_dynamic-update-slice_fusion.held_ref), channel_id=1, source_target_pairs={{0,4},{1,5},{2,6},{3,7},{4,0},{5,1},{6,2},{7,3},{8,12},{9,13},{10,... | collective-permute-start | bytes 122888 | tf_op jit(solution)/shard_map/ppermute | solution.py:124
  38.0 25.0 %all-to-all-start.1 = ((bf16[8,56,2048]{2,1,0:T(8,128)(2,1)}), bf16[8,56,2048]{2,1,0:T(8,128)(2,1)}, u32[]{:S(2)}, u32[]{:S(2)}) async-start(bf16[8,56,2048]{2,1,0:T(8,128)(2,1)} %bitcast.34), calls=%async_computation.1 | async-start | bytes 3670016 | tf_op jit(solution)/shard_map/all_to_all | solution.py:154
  46.8 0.8 copy-start.1
  47.6 29.5 %collective-permute-start.4 = (bf16[80,2048]{1,0:T(8,128)(2,1)}, bf16[80,2048]{1,0:T(8,128)(2,1)}, u32[]{:S(2)}, u32[]{:S(2)}) collective-permute-start(bf16[80,2048]{1,0:T(8,128)(2,1)} %get-tuple-element.31), channel_id=1, source_target_pairs={{0,1},{1,2},{2,3},{3,4},{4,5},{5,6},{6,7},{7,0},{8,9},{9,10},{10,1... | collective-permute-start | bytes 983048 | tf_op jit(solution)/shard_map/ppermute | solution.py:124
  51.9 25.2 %collective-permute-start.5 = (bf16[80,2048]{1,0:T(8,128)(2,1)}, bf16[80,2048]{1,0:T(8,128)(2,1)}, u32[]{:S(2)}, u32[]{:S(2)}) collective-permute-start(bf16[80,2048]{1,0:T(8,128)(2,1)} %get-tuple-element.32), channel_id=1, source_target_pairs={{0,7},{1,0},{2,1},{3,2},{4,3},{5,4},{6,5},{7,6},{8,15},{9,8},{10,9... | collective-permute-start | bytes 983048 | tf_op jit(solution)/shard_map/ppermute | solution.py:124
  54.1 19.5 %collective-permute-start.6 = (bf16[40,2048]{1,0:T(8,128)(2,1)S(1)}, bf16[40,2048]{1,0:T(8,128)(2,1)}, u32[]{:S(2)}, u32[]{:S(2)}) collective-permute-start(bf16[40,2048]{1,0:T(8,128)(2,1)S(1)} %get-tuple-element.33), channel_id=1, source_target_pairs={{0,2},{1,3},{2,4},{3,5},{4,6},{5,7},{6,0},{7,1},{64,70},{65,71},{6... | collective-permute-start | bytes 491528 | tf_op jit(solution)/shard_map/ppermute | solution.py:130
  63.0 14.1 %copy-start.2 = (bf16[120,2048]{1,0:T(8,128)(2,1)S(1)}, bf16[120,2048]{1,0:T(8,128)(2,1)}, u32[]{:S(2)}) copy-start(bf16[120,2048]{1,0:T(8,128)(2,1)} %copy-done.1) | copy-start | bytes 1474564
  63.0 30.6 %copy-start.3 = (bf16[1,40,2048]{2,1,0:T(8,128)(2,1)S(1)}, bf16[1,40,2048]{2,1,0:T(8,128)(2,1)}, u32[]{:S(2)}) copy-start(bf16[1,40,2048]{2,1,0:T(8,128)(2,1)} %param.8) | copy-start | bytes 491524
  63.0 45.5 %copy-start.4 = (bf16[1,40,2048]{2,1,0:T(8,128)(2,1)S(1)}, bf16[1,40,2048]{2,1,0:T(8,128)(2,1)}, u32[]{:S(2)}) copy-start(bf16[1,40,2048]{2,1,0:T(8,128)(2,1)} %param.9) | copy-start | bytes 491524
  66.4 19.6 %collective-permute-start.12 = (bf16[40,2048]{1,0:T(8,128)(2,1)S(1)}, bf16[40,2048]{1,0:T(8,128)(2,1)S(1)}, u32[]{:S(2)}, u32[]{:S(2)}) collective-permute-start(bf16[40,2048]{1,0:T(8,128)(2,1)S(1)} %get-tuple-element.39), channel_id=1, source_target_pairs={{0,2},{1,3},{2,4},{3,5},{4,6},{5,7},{6,0},{7,1},{64,70},{65,71},{6... | collective-permute-start | bytes 491528 | tf_op jit(solution)/shard_map/ppermute | solution.py:130
  70.6 15.4 %collective-permute-start.10 = (bf16[80,2048]{1,0:T(8,128)(2,1)S(1)}, bf16[80,2048]{1,0:T(8,128)(2,1)S(1)}, u32[]{:S(2)}, u32[]{:S(2)}) collective-permute-start(bf16[80,2048]{1,0:T(8,128)(2,1)S(1)} %get-tuple-element.37), channel_id=1, source_target_pairs={{0,1},{1,2},{2,3},{3,4},{4,5},{5,6},{6,7},{7,0},{8,9},{9,10},{10,1... | collective-permute-start | bytes 983048 | tf_op jit(solution)/shard_map/ppermute | solution.py:124
  73.6 12.4 %collective-permute-start.11 = (bf16[80,2048]{1,0:T(8,128)(2,1)S(1)}, bf16[80,2048]{1,0:T(8,128)(2,1)S(1)}, u32[]{:S(2)}, u32[]{:S(2)}) collective-permute-start(bf16[80,2048]{1,0:T(8,128)(2,1)S(1)} %get-tuple-element.38), channel_id=1, source_target_pairs={{0,7},{1,0},{2,1},{3,2},{4,3},{5,4},{6,5},{7,6},{8,15},{9,8},{10,9... | collective-permute-start | bytes 983048 | tf_op jit(solution)/shard_map/ppermute | solution.py:124
  78.3 15.2 %collective-permute-start.7 = (bf16[40,2048]{1,0:T(8,128)(2,1)S(1)}, bf16[40,2048]{1,0:T(8,128)(2,1)S(1)}, u32[]{:S(2)}, u32[]{:S(2)}) collective-permute-start(bf16[40,2048]{1,0:T(8,128)(2,1)S(1)} %get-tuple-element.42), channel_id=1, source_target_pairs={{0,2},{1,3},{2,4},{3,5},{4,6},{5,7},{6,0},{7,1},{8,10},{9,11},{10,... | collective-permute-start | bytes 491528 | tf_op jit(solution)/shard_map/ppermute | solution.py:124
  80.3 13.3 %collective-permute-start.8 = (bf16[40,2048]{1,0:T(8,128)(2,1)S(1)}, bf16[40,2048]{1,0:T(8,128)(2,1)S(1)}, u32[]{:S(2)}, u32[]{:S(2)}) collective-permute-start(bf16[40,2048]{1,0:T(8,128)(2,1)S(1)} %get-tuple-element.43), channel_id=1, source_target_pairs={{0,6},{1,7},{2,0},{3,1},{4,2},{5,3},{6,4},{7,5},{8,14},{9,15},{10,... | collective-permute-start | bytes 491528 | tf_op jit(solution)/shard_map/ppermute | solution.py:124
  86.2 22.4 %collective-permute-start.13 = (bf16[40,2048]{1,0:T(8,128)(2,1)S(1)}, bf16[40,2048]{1,0:T(8,128)(2,1)S(1)}, u32[]{:S(2)}, u32[]{:S(2)}) collective-permute-start(bf16[40,2048]{1,0:T(8,128)(2,1)S(1)} %get-tuple-element.40), channel_id=1, source_target_pairs={{0,2},{1,3},{2,4},{3,5},{4,6},{5,7},{6,0},{7,1},{8,10},{9,11},{10,... | collective-permute-start | bytes 491528 | tf_op jit(solution)/shard_map/ppermute | solution.py:124
  89.3 19.2 %collective-permute-start.14 = (bf16[40,2048]{1,0:T(8,128)(2,1)S(1)}, bf16[40,2048]{1,0:T(8,128)(2,1)S(1)}, u32[]{:S(2)}, u32[]{:S(2)}) collective-permute-start(bf16[40,2048]{1,0:T(8,128)(2,1)S(1)} %get-tuple-element.41), channel_id=1, source_target_pairs={{0,6},{1,7},{2,0},{3,1},{4,2},{5,3},{6,4},{7,5},{8,14},{9,15},{10,... | collective-permute-start | bytes 491528 | tf_op jit(solution)/shard_map/ppermute | solution.py:124
  94.7 17.0 %collective-permute-start.9 = (bf16[40,2048]{1,0:T(8,128)(2,1)S(1)}, bf16[40,2048]{1,0:T(8,128)(2,1)S(1)}, u32[]{:S(2)}, u32[]{:S(2)}) collective-permute-start(bf16[40,2048]{1,0:T(8,128)(2,1)S(1)} %add_convert_fusion.3), channel_id=1, source_target_pairs={{0,64},{64,128},{128,192},{192,256},{256,320},{320,384},{384,448},... | collective-permute-start | bytes 491528 | tf_op jit(solution)/shard_map/ppermute | solution.py:124
  108.7 8.5 %collective-permute-start.15 = (bf16[40,2048]{1,0:T(8,128)(2,1)S(1)}, bf16[40,2048]{1,0:T(8,128)(2,1)S(1)}, u32[]{:S(2)}, u32[]{:S(2)}) collective-permute-start(bf16[40,2048]{1,0:T(8,128)(2,1)S(1)} %add_convert_fusion), channel_id=1, source_target_pairs={{0,448},{64,0},{128,64},{192,128},{256,192},{320,256},{384,320},{4... | collective-permute-start | bytes 491528 | tf_op jit(solution)/shard_map/ppermute | solution.py:124
